TPU v7x, 1024 devices: a whole 4x4x32 slice. The times are simulated.
1024 devices in a mesh: dom: 128 (over z, x), grp: 8 (over y, core).
Axes of the slice: x: 4, y: 4, z: 32, core: 2. Of those that a mesh axis runs over, the one named last changes fastest.
Arguments:
- leaves: float32 [65536, 4, 128], P(('dom', 'grp')), as said below
- counts: int32 [65536], P(('dom', 'grp')), may hold values from 32 to 128, as said below
- send_list: int32 [1024, 8, 8], P(('dom', 'grp')), may hold values from 0 to 63
- pair_list: int32 [1024, 2, 128], P(('dom', 'grp')), may hold values from 0 to 63, as said below
- multipoles: float32 [35, 65536], P(None, ('dom', 'grp')), may hold values from -6 to 6
- far_list: int32 [1024, 3, 2048], P(('dom', 'grp')), may hold values from 0 to 8191, as said below
- trans_ops: float32 [35, 35, 256], replicated, may hold values from -0.1875 to 0.1875
Outputs:
- forces: float32 [65536, 3, 128], P(('dom', 'grp'))
- local_exp: float32 [35, 65536], P(None, ('dom', 'grp'))
Inputs may be any that keep to these rules, and one draw needn't show every extreme that they name: `counts`: the largest count appears in every device's blocks. `pair_list`: each received slot is named by exactly two pairs of a device. `far_list`: each target cell is named by exactly 32 pairs of a device; sources lie below 8192 and classes below 256. `leaves`: positions within 0 and 1, masses positive.
All inputs are finite; a program needn't handle non-finite values.
Results may differ from a plain program's by a relative error of at most 0.000076.
Values sent between devices are 32-bit elements; how exact they have to be, the bound alone decides.
No kernel may reach another device: no remote copies, remote signals or barrier semaphores. Data moves between devices by JAX's collectives and lax.ppermute only.
A program may use at most 64 MiB of HBM per device.

v0:
```python
import math

import jax
import jax.numpy as jnp
from jax import lax
from jax.sharding import PartitionSpec as P

SOFTEN = 0.04


def pair_forces(block_a, block_b):
    delta = block_b[:, :3, None, :] - block_a[:, :3, :, None]
    dist = jnp.sum(delta * delta, axis=1) + SOFTEN
    weight = dist ** (-1.5)
    force_a = jnp.sum(delta * (block_b[:, 3, None, :] * weight)[:, None], axis=3)
    second_force = -jnp.sum(delta * (block_a[:, 3, :, None] * weight)[:, None], axis=2)
    return (force_a, second_force)


def slot_selector(index, length):
    return (index[None, :] == jnp.arange(length, dtype=jnp.int32)[:, None]).astype(jnp.float32)


def shards(leaves, counts, send_list, pair_list, multipoles, far_list, trans_ops):
    leaf_dev, _, block_width = leaves.shape
    live = (jnp.arange(block_width, dtype=jnp.int32)[None, :] < counts[:, None]).astype(jnp.float32)
    masked = jnp.concatenate([leaves[:, :3], leaves[:, 3:4] * live[:, None, :]], axis=1)
    table = send_list[0]
    group_partners, count_of_slots = table.shape
    number_slots = group_partners * count_of_slots
    outgoing = jnp.take(masked, table, axis=0)
    received = lax.all_to_all(outgoing, "grp", split_axis=0, concat_axis=0, tiled=True).reshape(
        number_slots, 4, block_width
    )
    leaf_idx = pair_list[0, 0]
    slot_index = pair_list[0, 1]
    npairs = leaf_idx.shape[0]
    step_rows = math.gcd(16, npairs)

    def tile_forces(indices):
        return pair_forces(
            jnp.take(masked, indices[0], axis=0), jnp.take(received, indices[1], axis=0)
        )

    force_a, second_force = lax.map(
        tile_forces, (leaf_idx.reshape(-1, step_rows), slot_index.reshape(-1, step_rows))
    )
    force_a = force_a.reshape(npairs, 3 * block_width)
    second_force = second_force.reshape(npairs, 3 * block_width)
    own = jnp.dot(slot_selector(leaf_idx, leaf_dev), force_a, precision=lax.Precision.HIGHEST)
    force_per_slot = jnp.dot(
        slot_selector(slot_index, number_slots), second_force, precision=lax.Precision.HIGHEST
    )
    returned_forces = lax.all_to_all(
        force_per_slot.reshape(group_partners, count_of_slots, 3 * block_width),
        "grp",
        split_axis=0,
        concat_axis=0,
        tiled=True,
    )
    returned_forces = returned_forces.reshape(number_slots, 3 * block_width)
    total = own + jnp.dot(
        slot_selector(table.reshape(-1), leaf_dev), returned_forces, precision=lax.Precision.HIGHEST
    )
    forces = total.reshape(leaf_dev, 3, block_width) * live[:, None, :]
    entries = far_list[0]
    target = entries[0]
    source = entries[1]
    klass = entries[2]
    ncoef, cells_dev = multipoles.shape
    column = lax.all_gather(multipoles, "dom", axis=1, tiled=True)
    picked = jnp.take(column, source, axis=1)
    nfar = source.shape[0]
    group_rows = math.gcd(256, nfar)

    def translate_group(items):
        ops = jnp.take(trans_ops, items[0], axis=2)
        return jnp.einsum("jkp,pk->pj", ops, items[1], precision=lax.Precision.HIGHEST)

    translated = lax.map(
        translate_group, (klass.reshape(-1, group_rows), picked.T.reshape(-1, group_rows, ncoef))
    )
    translated = translated.reshape(nfar, ncoef)
    local = jnp.dot(slot_selector(target, cells_dev), translated, precision=lax.Precision.HIGHEST)
    return (forces, local.T)


def solution(mesh):
    return jax.shard_map(
        shards,
        mesh=mesh,
        in_specs=(
            P(("dom", "grp"), None, None),
            P(("dom", "grp")),
            P(("dom", "grp"), None, None),
            P(("dom", "grp"), None, None),
            P(None, ("dom", "grp")),
            P(("dom", "grp"), None, None),
            P(),
        ),
        out_specs=(P(("dom", "grp"), None, None), P(None, ("dom", "grp"))),
        check_vma=False,
    )
```

profile of v0, /device:TPU:8, one launch (start us, length us, event | category | flops | bytes accessed | tf_op | source)
XLA Modules:
  0.0 449.7 jit_solution(11757196544074279604)
XLA Ops:
  12.1 16.4 %all-to-all-start = ((f32[8,8,4,128]{3,2,1,0:T(4,128)}), f32[8,8,4,128]{3,2,1,0:T(4,128)S(1)}, u32[]{:S(2)}, u32[]{:S(2)}) async-start(f32[8,8,4,128]{3,2,1,0:T(4,128)} %broadcast_select_fusion.3), calls=%async_computation | async-start | bytes 262144 | tf_op jit(solution)/shard_map/all_to_all | solution.py:32
  33.1 6.0 %copy.18 = f32[35,35,256]{1,0,2:T(8,128)} copy(f32[35,35,256]{2,1,0:T(8,128)} %param.19) | data formatting | bytes 2508800 | tf_op jit(solution)/shard_map/while | solution.py:80
  39.1 40.2 %while.22 = (s32[]{:T(128)}, f32[8,16,3,128]{3,2,1,0:T(4,128)S(1)}, f32[8,16,3,128]{3,2,1,0:T(4,128)S(1)}, s32[8,16]{1,0:T(8,128)S(1)}, f32[64,4,128]{2,1,0:T(4,...) while((s32[]{:T(128)}, f32[8,16,3,128]{3,2,1,0:T(4,128)S(1)}, ...), condition=%wide.region_4.6_spmd, body=%wide.region_0.5_spmd.sunk | while | flops 6828226 | bytes 6890145 | solution.py:45
  80.3 4.8 %all-to-all-start.1 = ((f32[8,8,384]{2,1,0:T(8,128)}), f32[8,8,384]{2,1,0:T(8,128)S(1)}, u32[]{:S(2)}, u32[]{:S(2)}) async-start(f32[8,8,384]{2,1,0:T(8,128)} %fusion.20), calls=%async_computation.1 | async-start | bytes 196608 | tf_op jit(solution)/shard_map/all_to_all | solution.py:54
  90.4 207.8 %all-gather.3.cloned.1.call-done = f32[128,64,35]{1,2,0:T(8,128)} async-done(((f32[1,64,35]{1,2,0:T(8,128)}), f32[128,64,35]{1,2,0:T(8,128)}) %all-gather.3.cloned.1.call-update) | async-done | bytes 1146896 | tf_op jit(solution)/shard_map/all_gather | solution.py:71
  298.2 5.1 %copy.17 = f32[128,64,35]{2,1,0:T(8,128)} copy(f32[128,64,35]{1,2,0:T(8,128)} %all-gather.3.cloned.1.call-done) | data formatting | bytes 2293760 | tf_op jit(solution)/shard_map/all_gather | solution.py:71
  303.4 7.6 %gather_fusion.4 = f32[2048,35]{1,0:T(8,128)S(1)} fusion(f32[35,8192]{0,1:T(8,128)} %bitcast.99, s32[2048]{0:T(1024)S(1)} %broadcast_clamp_fusion), kind=kCustom, calls=%fused_computation.4 | custom fusion | bytes 581632 | tf_op jit(solution)/shard_map/jit(_take)/gather | solution.py:72
  311.4 129.9 %while.23 = (s32[]{:T(128)}, f32[8,256,35]{2,1,0:T(8,128)S(1)}, s32[8,256]{1,0:T(8,128)S(1)}, f32[35,35,256]{1,0,2:T(8,128)}, f32[8,256,35]{2,1,0:T(8,128)S(1)}, /*index=5*/s32[]{:T(128)}) while((s32[]{:T(128)}, f32[8,256,35]{2,1,0:T(8,128)S(1)}, s32[8,256]{1,0:T(8,128)S(1)}, f32[35,35,256]{1,0,2:T(8,128)}, f32[8,256,35]{2,1,0:T(8,128)S(1)}, ...), condition=%wide.region_6.8_spmd, body=%wide.region_5.7_spmd.sunk | while | flops 4080130 | bytes 4179537 | solution.py:80
  311.4 5.7 %gather_fusion.2 = f32[256,35,35]{2,1,0:T(8,128)} fusion(f32[35,35,256]{1,0,2:T(8,128)} %get-tuple-element.272, s32[1024]{0:T(1024)S(1)} %pad_clamp_fusion.9), kind=kCustom, calls=%fused_computation.1.clone.1 | custom fusion | bytes 2509824 | tf_op jit(solution)/shard_map/while/body/eval_jaxpr/jit(_take)/gather | solution.py:77
  317.2 10.4 %fusion.41 = f32[256,1,35]{2,1,0:T(1,128)S(1)} fusion(f32[256,35,1]{1,2,0:T(1,128)S(1)} %bitcast.98, f32[256,35,35]{2,1,0:T(8,128)} %gather_fusion.2, pred[256]{0:T(512)(128)(4,1)S(1)} %compare_and_fusion.10), kind=kOutput, calls=%fused_computation.5.clone.1 | convolution fusion | flops 4076800 | bytes 1326336 | tf_op jit(solution)/shard_map/while/body/eval_jaxpr/jkp,pk->pj/dot_general | solution.py:78
  327.6 5.7 %gather_fusion.2 = f32[256,35,35]{2,1,0:T(8,128)} fusion(f32[35,35,256]{1,0,2:T(8,128)} %get-tuple-element.272, s32[1024]{0:T(1024)S(1)} %pad_clamp_fusion.9), kind=kCustom, calls=%fused_computation.1.clone.1 | custom fusion | bytes 2509824 | tf_op jit(solution)/shard_map/while/body/eval_jaxpr/jit(_take)/gather | solution.py:77
  333.4 10.4 %fusion.41 = f32[256,1,35]{2,1,0:T(1,128)S(1)} fusion(f32[256,35,1]{1,2,0:T(1,128)S(1)} %bitcast.98, f32[256,35,35]{2,1,0:T(8,128)} %gather_fusion.2, pred[256]{0:T(512)(128)(4,1)S(1)} %compare_and_fusion.10), kind=kOutput, calls=%fused_computation.5.clone.1 | convolution fusion | flops 4076800 | bytes 1326336 | tf_op jit(solution)/shard_map/while/body/eval_jaxpr/jkp,pk->pj/dot_general | solution.py:78
  343.9 5.7 %gather_fusion.2 = f32[256,35,35]{2,1,0:T(8,128)} fusion(f32[35,35,256]{1,0,2:T(8,128)} %get-tuple-element.272, s32[1024]{0:T(1024)S(1)} %pad_clamp_fusion.9), kind=kCustom, calls=%fused_computation.1.clone.1 | custom fusion | bytes 2509824 | tf_op jit(solution)/shard_map/while/body/eval_jaxpr/jit(_take)/gather | solution.py:77
  349.6 10.4 %fusion.41 = f32[256,1,35]{2,1,0:T(1,128)S(1)} fusion(f32[256,35,1]{1,2,0:T(1,128)S(1)} %bitcast.98, f32[256,35,35]{2,1,0:T(8,128)} %gather_fusion.2, pred[256]{0:T(512)(128)(4,1)S(1)} %compare_and_fusion.10), kind=kOutput, calls=%fused_computation.5.clone.1 | convolution fusion | flops 4076800 | bytes 1326336 | tf_op jit(solution)/shard_map/while/body/eval_jaxpr/jkp,pk->pj/dot_general | solution.py:78
  360.1 5.7 %gather_fusion.2 = f32[256,35,35]{2,1,0:T(8,128)} fusion(f32[35,35,256]{1,0,2:T(8,128)} %get-tuple-element.272, s32[1024]{0:T(1024)S(1)} %pad_clamp_fusion.9), kind=kCustom, calls=%fused_computation.1.clone.1 | custom fusion | bytes 2509824 | tf_op jit(solution)/shard_map/while/body/eval_jaxpr/jit(_take)/gather | solution.py:77
  365.9 10.4 %fusion.41 = f32[256,1,35]{2,1,0:T(1,128)S(1)} fusion(f32[256,35,1]{1,2,0:T(1,128)S(1)} %bitcast.98, f32[256,35,35]{2,1,0:T(8,128)} %gather_fusion.2, pred[256]{0:T(512)(128)(4,1)S(1)} %compare_and_fusion.10), kind=kOutput, calls=%fused_computation.5.clone.1 | convolution fusion | flops 4076800 | bytes 1326336 | tf_op jit(solution)/shard_map/while/body/eval_jaxpr/jkp,pk->pj/dot_general | solution.py:78
  376.4 5.7 %gather_fusion.2 = f32[256,35,35]{2,1,0:T(8,128)} fusion(f32[35,35,256]{1,0,2:T(8,128)} %get-tuple-element.272, s32[1024]{0:T(1024)S(1)} %pad_clamp_fusion.9), kind=kCustom, calls=%fused_computation.1.clone.1 | custom fusion | bytes 2509824 | tf_op jit(solution)/shard_map/while/body/eval_jaxpr/jit(_take)/gather | solution.py:77
  382.1 10.4 %fusion.41 = f32[256,1,35]{2,1,0:T(1,128)S(1)} fusion(f32[256,35,1]{1,2,0:T(1,128)S(1)} %bitcast.98, f32[256,35,35]{2,1,0:T(8,128)} %gather_fusion.2, pred[256]{0:T(512)(128)(4,1)S(1)} %compare_and_fusion.10), kind=kOutput, calls=%fused_computation.5.clone.1 | convolution fusion | flops 4076800 | bytes 1326336 | tf_op jit(solution)/shard_map/while/body/eval_jaxpr/jkp,pk->pj/dot_general | solution.py:78
  392.6 5.7 %gather_fusion.2 = f32[256,35,35]{2,1,0:T(8,128)} fusion(f32[35,35,256]{1,0,2:T(8,128)} %get-tuple-element.272, s32[1024]{0:T(1024)S(1)} %pad_clamp_fusion.9), kind=kCustom, calls=%fused_computation.1.clone.1 | custom fusion | bytes 2509824 | tf_op jit(solution)/shard_map/while/body/eval_jaxpr/jit(_take)/gather | solution.py:77
  398.4 10.4 %fusion.41 = f32[256,1,35]{2,1,0:T(1,128)S(1)} fusion(f32[256,35,1]{1,2,0:T(1,128)S(1)} %bitcast.98, f32[256,35,35]{2,1,0:T(8,128)} %gather_fusion.2, pred[256]{0:T(512)(128)(4,1)S(1)} %compare_and_fusion.10), kind=kOutput, calls=%fused_computation.5.clone.1 | convolution fusion | flops 4076800 | bytes 1326336 | tf_op jit(solution)/shard_map/while/body/eval_jaxpr/jkp,pk->pj/dot_general | solution.py:78
  408.8 5.7 %gather_fusion.2 = f32[256,35,35]{2,1,0:T(8,128)} fusion(f32[35,35,256]{1,0,2:T(8,128)} %get-tuple-element.272, s32[1024]{0:T(1024)S(1)} %pad_clamp_fusion.9), kind=kCustom, calls=%fused_computation.1.clone.1 | custom fusion | bytes 2509824 | tf_op jit(solution)/shard_map/while/body/eval_jaxpr/jit(_take)/gather | solution.py:77
  414.6 10.4 %fusion.41 = f32[256,1,35]{2,1,0:T(1,128)S(1)} fusion(f32[256,35,1]{1,2,0:T(1,128)S(1)} %bitcast.98, f32[256,35,35]{2,1,0:T(8,128)} %gather_fusion.2, pred[256]{0:T(512)(128)(4,1)S(1)} %compare_and_fusion.10), kind=kOutput, calls=%fused_computation.5.clone.1 | convolution fusion | flops 4076800 | bytes 1326336 | tf_op jit(solution)/shard_map/while/body/eval_jaxpr/jkp,pk->pj/dot_general | solution.py:78
  425.1 5.7 %gather_fusion.2 = f32[256,35,35]{2,1,0:T(8,128)} fusion(f32[35,35,256]{1,0,2:T(8,128)} %get-tuple-element.272, s32[1024]{0:T(1024)S(1)} %pad_clamp_fusion.9), kind=kCustom, calls=%fused_computation.1.clone.1 | custom fusion | bytes 2509824 | tf_op jit(solution)/shard_map/while/body/eval_jaxpr/jit(_take)/gather | solution.py:77
  430.8 10.4 %fusion.41 = f32[256,1,35]{2,1,0:T(1,128)S(1)} fusion(f32[256,35,1]{1,2,0:T(1,128)S(1)} %bitcast.98, f32[256,35,35]{2,1,0:T(8,128)} %gather_fusion.2, pred[256]{0:T(512)(128)(4,1)S(1)} %compare_and_fusion.10), kind=kOutput, calls=%fused_computation.5.clone.1 | convolution fusion | flops 4076800 | bytes 1326336 | tf_op jit(solution)/shard_map/while/body/eval_jaxpr/jkp,pk->pj/dot_general | solution.py:78
  (187 shorter events, 57.5 us)
Async XLA Ops:
  12.1 27.0 %all-to-all-start = ((f32[8,8,4,128]{3,2,1,0:T(4,128)}), f32[8,8,4,128]{3,2,1,0:T(4,128)S(1)}, u32[]{:S(2)}, u32[]{:S(2)}) async-start(f32[8,8,4,128]{3,2,1,0:T(4,128)} %broadcast_select_fusion.3), calls=%async_computation | async-start | bytes 262144 | tf_op jit(solution)/shard_map/all_to_all | solution.py:32
  28.5 269.8 %all-gather.3.cloned.1.call-start = ((), (), s32[]{:S(2)}) async-start(), calls=%async_computation.2 | async-start | bytes 2641920 | tf_op jit(solution)/shard_map/all_gather | solution.py:71
  80.3 9.2 %all-to-all-start.1 = ((f32[8,8,384]{2,1,0:T(8,128)}), f32[8,8,384]{2,1,0:T(8,128)S(1)}, u32[]{:S(2)}, u32[]{:S(2)}) async-start(f32[8,8,384]{2,1,0:T(8,128)} %fusion.20), calls=%async_computation.1 | async-start | bytes 196608 | tf_op jit(solution)/shard_map/all_to_all | solution.py:54
Sparse Core Ops, SparseCore 0:
  33.4 264.7 all-gather.2
where the time goes:
time: 451 us; the launch traced here: 450 us
  waiting for transfers between devices  213 us (47%)
  matrix products  86 us (19%)
  local copies, waits for them, and re-layouts  78.4 us (17%)
  other arithmetic  36 us (8%)
  starting transfers between devices  21.2 us (5%)
  between operations  14.1 us (3%)
    all_gather x1, waiting for transfers between devices, shards(): column = lax.all_gather(multipoles, 'dom', axis=1, tiled=True)  208 us
    dot_general x8, matrix products, translate_group(): jnp.einsum('jkp,pk->pj', ops, items[1], precision=lax.Precision.HIGHEST)  83.2 us
    gather x8, local copies, waits for them, and re-layouts, translate_group(): ops = jnp.take(trans_ops, items[0], axis=2)  45.9 us
    all_to_all x1, starting transfers between devices, shards(): lax.all_to_all(outgoing, 'grp', split_axis=0, concat_axis=0, tiled=True)  16.4 us
    reduce_sum x8, other arithmetic, pair_forces(): jnp.sum(delta * (block_a[:, 3, :, None] * weight)[:, None], axis=2)  15.7 us
  transfers between devices with their start and end apart: 3, of which 2 were waited for; matrix products, arithmetic and copies ran while one was open for 11% of the time, Pallas kernels for 0%

commit v1 on v0

v1 whole, which is shorter than its diff:
```python
import jax
import jax.numpy as jnp
from jax import lax
from jax.experimental import pallas as pl
from jax.experimental.pallas import tpu as pltpu
from jax.sharding import Mesh, PartitionSpec as P

SOFTEN = 0.04
F32 = jnp.float32
BF16 = jnp.bfloat16
NCOEF = 35
STRIDE = 40
NGROUP = 48
TILE = 64
NTILE = 80
ROWS = NTILE * TILE
CHUNK = 8
BATCH = 8
MOVES = 32
NFAR = 2048
LEAF = 64
PAIRS = 128
TABLE = 8192

VMEM = pl.BlockSpec(memory_space=pltpu.VMEM)
SMEM = pl.BlockSpec(memory_space=pltpu.SMEM)
ANY = pl.BlockSpec(memory_space=pl.ANY)


def params(mb=32):
    return pltpu.CompilerParams(vmem_limit_bytes=mb * 2**20)


def lanes(shape):
    return lax.broadcasted_iota(jnp.int32, shape, len(shape) - 1)


def rows(shape):
    return lax.broadcasted_iota(jnp.int32, shape, len(shape) - 2)


def pack_kernel(leaves, counts, send, out):
    lane, row = lanes((4, 128)), rows((4, 128))

    def step(k, _):
        l = send[k]
        dead = (row == 3) & (lane >= counts[l])
        out[k] = jnp.where(dead, 0.0, leaves[l])
        return 0

    lax.fori_loop(0, LEAF, step, 0, unroll=8)


def split(x):
    h = x.astype(BF16)
    r = x - h.astype(F32)
    m = r.astype(BF16)
    return h, m, (r - m.astype(F32)).astype(BF16)


def split_rows(x):
    return [p.astype(F32) for p in split(x)]


def pair_kernel(pairs, counts, leaves, received, own, slot, a_dist, b_dist, a_sums, b_sums, a_pos, b_pos, a_cen, b_cen,
                filled, named):
    lane, row = lanes((4, 128)), rows((4, 128))
    one, zero = jnp.ones((1, 128), F32), jnp.zeros((3, 128), F32)
    own[...] = jnp.zeros_like(own)

    def sums_of(block):
        pos, mass = block[0:3], block[3:4]
        centre = jnp.broadcast_to(pos[:, 0:1], (3, 128))
        weighted = jnp.concatenate([(pos - centre) * mass, mass, one * 0.0, zero], axis=0)
        parts = split_rows(weighted)
        stacked = jnp.concatenate(parts + [jnp.zeros((8, 128), F32)], axis=0).astype(BF16)
        return stacked, jnp.concatenate([centre, one * 0.0], axis=0)

    def operands(k):
        block = jnp.where((row == 3) & (lane >= counts[k]), 0.0, leaves[k])
        pos = block[0:3]
        square = jnp.sum(pos * pos, axis=0, keepdims=True)
        h, m, l = split_rows(jnp.concatenate([-2.0 * pos, square, one, zero], axis=0))
        near = jnp.concatenate([h, h, m, h, l, m], axis=0).astype(BF16)
        other = received[k]
        pos = other[0:3]
        square = jnp.sum(pos * pos, axis=0, keepdims=True) + SOFTEN
        h, m, l = split_rows(jnp.concatenate([pos, one, square, zero], axis=0))
        far = jnp.concatenate([h, m, h, l, h, m], axis=0).T.astype(BF16)
        return near, far, sums_of(block), sums_of(other), block, other

    def prepare(c, _):
        places = [c * BATCH + j for j in range(BATCH)]
        for k, done in zip(places, [operands(k) for k in places]):
            a_dist[k], b_dist[k], (a_sums[k], a_cen[k]), (b_sums[k], b_cen[k]), a_pos[k], b_pos[k] = done
            filled[k] = 0
        return 0

    lax.fori_loop(0, LEAF // BATCH, prepare, 0)

    def invert(p, _):
        q = pairs[PAIRS + p]
        n = filled[q]
        named[2 * q + n] = pairs[p]
        filled[q] = n + 1
        return 0

    lax.fori_loop(0, PAIRS, invert, 0, unroll=4)

    def gather_sum(s):
        return (s[0:8] + s[8:16] + s[16:24])[0:4]

    back = (((1,), (1,)), ((), ()))

    gap = jnp.zeros((32, 128), BF16)

    def forces_of(q, l, n):
        near = jnp.concatenate([a_dist[l], a_dist[n]], axis=1)
        dist = jnp.dot(b_dist[q], near, preferred_element_type=F32)
        r = lax.rsqrt(dist)
        w = r * r * r
        high = w.astype(BF16)
        low = (w - high.astype(F32)).astype(BF16)
        sb = b_sums[q]
        sa = jnp.concatenate(
            [jnp.concatenate([a_sums[l], gap], axis=1), jnp.concatenate([gap, a_sums[n]], axis=1)], axis=0
        )
        fb = lax.dot_general(sa, high, back, preferred_element_type=F32)
        fb = fb + lax.dot_general(sa, low, back, preferred_element_type=F32)
        fa = jnp.dot(sb, high, preferred_element_type=F32) + jnp.dot(sb, low, preferred_element_type=F32)
        bl, bn = gather_sum(fb[0:32]), gather_sum(fb[32:64])
        fl, fn = gather_sum(fa[:, 0:128]), gather_sum(fa[:, 128:256])
        back_force = bl - (b_pos[q] - a_cen[l]) * bl[3:4] + bn - (b_pos[q] - a_cen[n]) * bn[3:4]
        centre = b_cen[q]
        return back_force, fl - (a_pos[l] - centre) * fl[3:4], fn - (a_pos[n] - centre) * fn[3:4]

    def step(c, _):
        slots = [c * BATCH + j for j in range(BATCH)]
        leaves_of = [(named[2 * q], named[2 * q + 1]) for q in slots]
        results = [forces_of(q, l, n) for q, (l, n) in zip(slots, leaves_of)]
        for q, (l, n), (fb, fl, fn) in zip(slots, leaves_of, results):
            slot[q] = fb
            own[l] += fl
            own[n] += fn
        return 0

    lax.fori_loop(0, LEAF // BATCH, step, 0)


def finish_kernel(counts, send, own, back, out, total):
    total[...] = own[...]

    def add(k, _):
        total[send[k]] += back[k]
        return 0

    lax.fori_loop(0, LEAF, add, 0, unroll=4)
    lane = lanes((3, 128))

    def mask(l, _):
        out[l] = jnp.where(lane < counts[l], total[l][0:3], 0.0)
        return 0

    lax.fori_loop(0, LEAF, mask, 0, unroll=8)


def order_kernel(far, dst_out, row_out, tile_out, rows_out):
    blocks = NFAR // 128
    klass = far[2]
    source = far[1]
    place = (klass * 1366) >> 16
    group = klass - NGROUP * place
    wave = source >> 10
    row_out[...] = (
        (((source >> 6) & 3) * 16 + ((source >> 8) & 3) * 4 + (wave >> 1)) * 128
        + (wave & 1) * 64
        + (source & 63)
    )
    sub = rows((48, 128))
    before = (rows((128, 128)) < lanes((128, 128))).astype(F32).astype(BF16)
    count = jnp.zeros((48, 1), F32)
    picks, ranks = [], []
    for b in range(blocks):
        pick = (sub == group[b : b + 1]).astype(F32)
        rank = jnp.dot(pick.astype(BF16), before, preferred_element_type=F32) + count
        count = count + jnp.sum(pick, axis=1, keepdims=True)
        picks.append(pick)
        ranks.append(rank)
    tiles = ((count.astype(jnp.int32) + (TILE - 1)) >> 6).astype(F32)
    tiles = jnp.broadcast_to(tiles, (48, 128))
    lower = (lanes((48, 48)) < rows((48, 48))).astype(F32).astype(BF16)
    start = jnp.dot(lower, tiles.astype(BF16), preferred_element_type=F32)
    done = lanes((48, 128)).astype(F32) >= start + tiles
    which = jnp.sum(done.astype(F32), axis=0, keepdims=True).astype(jnp.int32)
    which = jnp.minimum(which, NGROUP - 1)
    used = jnp.sum(tiles, axis=0, keepdims=True).astype(jnp.int32)
    which = jnp.where(lanes((1, 128)) == NTILE, used, which)
    tile_out[...] = jnp.broadcast_to(which, (8, 128))
    for b in range(blocks):
        at = jnp.sum(picks[b] * (ranks[b] + start * TILE), axis=0, keepdims=True)
        dst_out[b : b + 1] = at.astype(jnp.int32)
        hot = (rows((64, 128)) == far[0][b : b + 1]).astype(F32)
        where = jnp.broadcast_to((place[b : b + 1] + 1).astype(F32), (64, 128))
        rows_out[b * 128 : (b + 1) * 128, :] = jnp.concatenate([hot, where], axis=0).T


def spread_kernel(dst, entries, select, slots, hot):
    hot[...] = jnp.zeros_like(hot)

    def step(c, _):
        some = [c * MOVES + j for j in range(MOVES)]
        found = [(dst[f], entries[pl.ds(f, 1), :]) for f in some]
        for d, value in found:
            hot[pl.ds(d, 1), :] = value
        return 0

    lax.fori_loop(0, NFAR // MOVES, step, 0)

    def turn(b, _):
        at = pl.multiple_of(b * 128, 128)
        part = hot[pl.ds(at, 128), :]
        slots[pl.ds(at, 128), :] = jnp.where(lanes((128, 128)) < 64, pltpu.roll(part, 64, 1), part)
        select[:, pl.ds(at, 128)] = part.T[0:64].astype(BF16)
        return 0

    lax.fori_loop(0, ROWS // 128, turn, 0, unroll=4)


def stack_kernel(ops, out, stacked):
    stacked[:, 104:256, :] = jnp.zeros((NGROUP, 152, 128), F32)
    pad = jnp.zeros((STRIDE - NCOEF, 256), F32)
    tail = jnp.zeros((128 - 3 * STRIDE, 256), F32)
    for s in range(6):
        for k in range(NCOEF, STRIDE):
            stacked[:, (s // 3) * 128 + (s % 3) * STRIDE + k, :] = jnp.zeros((NGROUP, 128), F32)
    same = (rows((256, 256)) == lanes((256, 256))).astype(F32).astype(BF16)
    for first in range(0, NCOEF, 5):
        turned = []
        for k in range(first, first + 5):
            parts = []
            for p in split_rows(ops[:, k, :]):
                parts += [p, pad]
            flat = jnp.concatenate(parts + [tail], axis=0).astype(BF16)
            turned.append(lax.dot_general(same, flat, (((1,), (1,)), ((), ())), preferred_element_type=F32))
        for k in range(5):
            for s in range(6):
                size = min(NGROUP, 256 - s * NGROUP)
                at = (s // 3) * 128 + (s % 3) * STRIDE + first + k
                stacked[0:size, at, :] = turned[k][s * NGROUP : s * NGROUP + size]

    def narrow(g, _):
        out[pl.ds(g * 4, 4)] = stacked[pl.ds(g * 4, 4), 0:256].astype(BF16)
        return 0

    lax.fori_loop(0, NGROUP // 4, narrow, 0)


def far_kernel(row, dst, tile, column, ops_hbm, slots_hbm, select_hbm, out,
               ops, slots, select, table, picked, sems):
    copies = [
        pltpu.make_async_copy(ops_hbm, ops, sems.at[0]),
        pltpu.make_async_copy(slots_hbm, slots, sems.at[1]),
        pltpu.make_async_copy(select_hbm, select, sems.at[2]),
    ]
    for c in copies:
        c.start()

    pad = jnp.zeros((4, 128), F32)
    tail = jnp.zeros((8, 128), F32)

    def turn(i, _):
        turned = []
        for p in range(2):
            both = column[pl.ds(pl.multiple_of(i * 144 + p * 72, 8), 72), :]
            for h in range(2):
                one = jnp.concatenate([both[36 * h : 36 * h + 36], pad], axis=0)
                turned.append(jnp.concatenate([one, one, one, tail], axis=0).T)
        for p, value in enumerate(turned):
            table[pl.ds(pl.multiple_of((4 * i + p) * 128, 128), 128), :] = value
        return 0

    lax.fori_loop(0, 16, turn, 0)

    def pick(c, _):
        some = [c * MOVES + j for j in range(MOVES)]
        found = [(dst[f], table[pl.ds(row[f], 1), :]) for f in some]
        for d, value in found:
            picked[pl.ds(d, 1), :] = value
        return 0

    lax.fori_loop(0, NFAR // MOVES, pick, 0)
    for c in copies:
        c.wait()

    lane = lanes((TILE, 128))
    place = (lane >= STRIDE).astype(F32) + (lane >= 2 * STRIDE).astype(F32) + 1.0
    left = jnp.where(lane < 3 * STRIDE, place, -1.0)
    right = jnp.where(lane < 3 * STRIDE, place + 3.0, -1.0)

    def translate(c, total):
        at = pl.multiple_of(c * (CHUNK * TILE), CHUNK * TILE)
        out_rows = []
        for j in range(CHUNK):
            here = pl.ds(pl.multiple_of(at + j * TILE, TILE), TILE)
            x = picked[here, :]
            s = slots[here, :]
            xl = split(jnp.where(s == left, x, 0.0))
            xr = split(jnp.where(s == right, x, 0.0))
            lhs = jnp.concatenate([jnp.concatenate([a, b], axis=1) for a, b in zip(xl, xr)], axis=0)
            y = jnp.dot(lhs, ops[tile[c * CHUNK + j]], preferred_element_type=F32)
            out_rows.append(y[0:TILE] + y[TILE : 2 * TILE] + y[2 * TILE :])
        moved = split(jnp.concatenate(out_rows, axis=0))
        chosen = select[:, pl.ds(at, CHUNK * TILE)]
        for part in moved:
            total = total + jnp.dot(chosen, part, preferred_element_type=F32)
        return total

    chunks = (tile[NTILE] + CHUNK - 1) // CHUNK
    total = lax.fori_loop(0, chunks, translate, jnp.zeros((64, 128), F32))
    flat = total.T
    out[...] = flat[0:NCOEF] + flat[STRIDE : STRIDE + NCOEF] + flat[2 * STRIDE : 2 * STRIDE + NCOEF]


def stacked_ops(trans_ops):
    return pl.pallas_call(
        stack_kernel, out_shape=jax.ShapeDtypeStruct((NGROUP, 256, 128), BF16),
        in_specs=[VMEM], out_specs=VMEM, scratch_shapes=[pltpu.VMEM((NGROUP, 264, 128), F32)],
        compiler_params=params(), cost_estimate=cost(10**9, 4 * 10**6), name="stack_operators",
    )(trans_ops)


def spread_out(block, axes, n):
    return lax.all_to_all(jnp.broadcast_to(block[None], (n,) + block.shape), axes, 0, 0, tiled=True)


def first_stage(multipoles):
    block = jnp.pad(multipoles, ((0, 1), (0, 0))).reshape(9, 2, 128)
    block = spread_out(block, "u", 8)
    return block.reshape(4, 2, 36, 64).transpose(0, 2, 1, 3).reshape(4, 9, 4, 128)


def cost(flops, size):
    return pl.CostEstimate(flops=flops, bytes_accessed=size, transcendentals=0)


def near_first(leaves, counts, send):
    return pl.pallas_call(
        pack_kernel, out_shape=jax.ShapeDtypeStruct((LEAF, 4, 128), F32),
        in_specs=[VMEM, SMEM, SMEM], out_specs=VMEM, compiler_params=params(),
        cost_estimate=cost(10**6, 10**6), name="pack_blocks",
    )(leaves, counts, send)


def near_pairs(leaves, counts, pairs, received):
    return pl.pallas_call(
        pair_kernel,
        out_shape=[jax.ShapeDtypeStruct((LEAF, 4, 128), F32)] * 2,
        in_specs=[SMEM, SMEM, VMEM, VMEM], out_specs=[VMEM] * 2,
        scratch_shapes=[
            pltpu.VMEM((LEAF, 48, 128), BF16), pltpu.VMEM((LEAF, 128, 48), BF16),
            pltpu.VMEM((LEAF, 32, 128), BF16), pltpu.VMEM((LEAF, 32, 128), BF16),
            pltpu.VMEM((LEAF, 4, 128), F32), pltpu.VMEM((LEAF, 4, 128), F32),
            pltpu.VMEM((LEAF, 4, 128), F32), pltpu.VMEM((LEAF, 4, 128), F32),
            pltpu.SMEM((LEAF,), jnp.int32), pltpu.SMEM((PAIRS,), jnp.int32),
        ],
        compiler_params=params(),
        cost_estimate=cost(10**9, 4 * 10**6), name="pair_forces",
    )(pairs, counts, leaves, received)


def near_last(counts, send, own, back):
    return pl.pallas_call(
        finish_kernel, out_shape=jax.ShapeDtypeStruct((LEAF, 3, 128), F32),
        in_specs=[SMEM, SMEM, VMEM, VMEM], out_specs=VMEM,
        scratch_shapes=[pltpu.VMEM((LEAF, 4, 128), F32)], compiler_params=params(),
        cost_estimate=cost(10**6, 10**6), name="add_returned",
    )(counts, send, own, back)


def far_order(far):
    dst, row, tile, entries = pl.pallas_call(
        order_kernel,
        out_shape=[jax.ShapeDtypeStruct((16, 128), jnp.int32), jax.ShapeDtypeStruct((16, 128), jnp.int32),
                   jax.ShapeDtypeStruct((8, 128), jnp.int32), jax.ShapeDtypeStruct((NFAR, 128), F32)],
        in_specs=[VMEM], out_specs=[VMEM] * 4, compiler_params=params(),
        cost_estimate=cost(10**8, 10**5), name="class_order",
    )(far.reshape(3, 16, 128))
    dst = dst.reshape(NFAR)
    select, slots = pl.pallas_call(
        spread_kernel,
        out_shape=[jax.ShapeDtypeStruct((64, ROWS), BF16), jax.ShapeDtypeStruct((ROWS, 128), F32)],
        in_specs=[SMEM, VMEM], out_specs=[VMEM] * 2,
        scratch_shapes=[pltpu.VMEM((ROWS, 128), F32)], compiler_params=params(),
        cost_estimate=cost(10**9, 4 * 10**6), name="sorted_targets",
    )(dst, entries)
    return dst, row.reshape(NFAR), tile[0], select, slots


def far_last(dst, row, tile, select, slots, ops, column):
    return pl.pallas_call(
        far_kernel, out_shape=jax.ShapeDtypeStruct((NCOEF, 64), F32),
        in_specs=[SMEM, SMEM, SMEM, VMEM, ANY, ANY, ANY], out_specs=VMEM,
        scratch_shapes=[
            pltpu.VMEM((NGROUP, 256, 128), BF16), pltpu.VMEM((ROWS, 128), F32), pltpu.VMEM((64, ROWS), BF16),
            pltpu.VMEM((TABLE, 128), F32), pltpu.VMEM((ROWS, 128), F32),
            pltpu.SemaphoreType.DMA((3,)),
        ],
        compiler_params=params(40), cost_estimate=cost(10**9, 8 * 10**6), name="translate",
    )(row, dst, tile, column, ops, slots, select)


def shards(leaves, counts, send_list, pair_list, multipoles, far_list, trans_ops):
    send = send_list.reshape(64)
    outgoing = near_first(leaves, counts, send).reshape(8, 8, 4, 128)
    received = lax.all_to_all(outgoing, "grp", 0, 0, tiled=True).reshape(64, 4, 128)
    own, slot = near_pairs(leaves, counts, pair_list.reshape(2 * PAIRS), received)
    back = lax.all_to_all(slot.reshape(8, 8, 4, 128), "grp", 0, 0, tiled=True).reshape(64, 4, 128)
    forces = near_last(counts, send, own, back)
    block = first_stage(multipoles)
    block, far_list = lax.optimization_barrier((block, far_list))
    block = spread_out(block, "v", 4).reshape(16, 9, 4, 128)
    dst, row, tile, select, slots = far_order(far_list[0])
    block, trans_ops, slots, select = lax.optimization_barrier((block, trans_ops, slots, select))
    block = spread_out(block, "x", 4)
    ops = stacked_ops(trans_ops)
    local = far_last(dst, row, tile, select, slots, ops, block.reshape(64 * 36, 128))
    return forces, local


def solution(mesh):
    fine = Mesh(mesh.devices.reshape(8, 4, 4, 8), ("u", "v", "x", "grp"))
    every = ("u", "v", "x", "grp")
    return jax.shard_map(
        shards,
        mesh=fine,
        in_specs=(P(every, None, None), P(every), P(every, None, None), P(every, None, None),
                  P(None, every), P(every, None, None), P()),
        out_specs=(P(every, None, None), P(None, every)),
        check_vma=False,
    )
```

time: 451 us -> 137 us (0.30)
  the two profiles are of different devices: /device:TPU:8 before, /device:TPU:1 now
where the time goes in v1:
time: 137 us; the launch traced here: 136 us
  starting transfers between devices  49.3 us (36%)
  Pallas kernels  45.6 us (33%)
  waiting for transfers between devices  27.3 us (20%)
  local copies, waits for them, and re-layouts  13.3 us (10%)
    all_to_all x3, starting transfers between devices, spread_out(): lax.all_to_all(jnp.broadcast_to(block[None], (n,) + block.shape), axes, 0...  36.8 us
    all_to_all x3, waiting for transfers between devices, spread_out(): lax.all_to_all(jnp.broadcast_to(block[None], (n,) + block.shape), axes, 0...  22.4 us
    pallas_call x1, Pallas kernels, near_pairs(): pl.pallas_call(pair_kernel, out_shape=[jax.ShapeDtypeStruct((LEAF, 4, 128...  17.3 us
    pallas_call x1, Pallas kernels, far_last(): pl.pallas_call(far_kernel, out_shape=jax.ShapeDtypeStruct((NCOEF, 64), F3...  11 us
    pallas_call x1, Pallas kernels, stacked_ops(): pl.pallas_call(stack_kernel, out_shape=jax.ShapeDtypeStruct((NGROUP, 256,...  9.92 us
    unnamed x23, local copies, waits for them, and re-layouts  8.78 us
    all_to_all x1, starting transfers between devices, shards(): lax.all_to_all(outgoing, 'grp', 0, 0, tiled=True).reshape(64, 4, 128)  8.36 us
    all_to_all x1, waiting for transfers between devices, shards(): lax.all_to_all(outgoing, 'grp', 0, 0, tiled=True).reshape(64, 4, 128)  4.89 us
  transfers between devices with their start and end apart: 5, of which 3 were waited for; matrix products, arithmetic and copies ran while one was open for 1% of the time, Pallas kernels for 25%

profile of v1, /device:TPU:1, one launch (start us, length us, event | category | flops | bytes accessed | tf_op | source)
XLA Modules:
  0.0 136.5 jit_solution(11459154031583431750)
XLA Ops:
  0.7 0.8 pad.4
  2.2 28.9 %all-to-all-start.2 = ((f32[8,9,2,128]{3,2,1,0:T(2,128)}), f32[8,9,2,128]{3,2,1,0:T(2,128)S(1)}, u32[]{:S(2)}, u32[]{:S(2)}) async-start(f32[8,9,2,128]{3,2,1,0:T(2,128)} %broadcast_in_dim.9), calls=%async_computation.2 | async-start | bytes 147456 | tf_op jit(solution)/shard_map/all_to_all | solution.py:333
  31.1 0.8 reshape.43.send
  31.8 0.9 copy-done.5
  33.4 1.3 pack_blocks.1
  34.7 18.9 %all-to-all-done.2 = f32[8,9,2,128]{3,2,1,0:T(2,128)S(1)} async-done(((f32[8,9,2,128]{3,2,1,0:T(2,128)}), f32[8,9,2,128]{3,2,1,0:T(2,128)S(1)}, u32[]{:S(2)}, u32[]{:S(2)}) %all-to-all-start.2) | async-done | bytes 73760 | tf_op jit(solution)/shard_map/all_to_all | solution.py:333
  53.6 8.4 %all-to-all-start = ((f32[8,8,4,128]{3,2,1,0:T(4,128)}), f32[8,8,4,128]{3,2,1,0:T(4,128)S(1)}, u32[]{:S(2)}, u32[]{:S(2)}) async-start(f32[8,8,4,128]{3,2,1,0:T(4,128)} %bitcast.1), calls=%async_computation | async-start | bytes 262144 | tf_op jit(solution)/shard_map/all_to_all | solution.py:415
  62.3 4.9 %all-to-all-done = f32[8,8,4,128]{3,2,1,0:T(4,128)S(1)} async-done(((f32[8,8,4,128]{3,2,1,0:T(4,128)}), f32[8,8,4,128]{3,2,1,0:T(4,128)S(1)}, u32[]{:S(2)}, u32[]{:S(2)}) %all-to-all-start) | async-done | bytes 131104 | tf_op jit(solution)/shard_map/all_to_all | solution.py:415
  67.2 0.8 broadcast_in_dim.10
  68.0 3.5 %all-to-all-start.3 = ((f32[4,4,9,4,128]{4,3,2,1,0:T(4,128)}), f32[4,4,9,4,128]{4,3,2,1,0:T(4,128)S(1)}, u32[]{:S(2)}, u32[]{:S(2)}) async-start(f32[4,4,9,4,128]{4,3,2,1,0:T(4,128)} %broadcast_in_dim.10), calls=%async_computation.3 | async-start | bytes 589824 | tf_op jit(solution)/shard_map/all_to_all | solution.py:333
  71.5 17.3 %pair_forces.1 = (f32[64,4,128]{2,1,0:T(4,128)S(1)}, f32[64,4,128]{2,1,0:T(4,128)}) custom-call(s32[256]{0:T(256)S(1)} %bitcast.19, s32[64]{0:T(128)S(1)} %copy-done.8, f32[64,4,128]{2,1,0:T(4,128)S(1)} %copy-done.6, f32[64,4,128]{2,1,0:T(4,128)S(1)} %bitcast.14), custom_call_target="tpu_custom_call" | custom-call | flops 1000000000 | bytes 4000000 | tf_op jit(solution)/shard_map/pair_forces/pallas_call | solution.py:355
  88.8 4.1 %all-to-all-start.1 = ((f32[8,8,4,128]{3,2,1,0:T(4,128)}), f32[8,8,4,128]{3,2,1,0:T(4,128)S(1)}, u32[]{:S(2)}, u32[]{:S(2)}) async-start(f32[8,8,4,128]{3,2,1,0:T(4,128)} %bitcast.3), calls=%async_computation.1 | async-start | bytes 262144 | tf_op jit(solution)/shard_map/all_to_all | solution.py:417
  93.4 4.7 %sorted_targets.1 = (bf16[64,5120]{1,0:T(8,128)(2,1)S(1)}, f32[5120,128]{1,0:T(8,128)S(1)}) custom-call(s32[2048]{0:T(1024)S(1)} %bitcast.15, f32[2048,128]{1,0:T(8,128)S(1)} %get-tuple-element.23.entries), custom_call_target="tpu_custom_call" | custom-call | flops 1000000000 | bytes 4000000 | tf_op jit(solution)/shard_map/sorted_targets/pallas_call | solution.py:389
  98.1 1.5 %copy-done = f32[5120,128]{1,0:T(8,128)} copy-done((f32[5120,128]{1,0:T(8,128)}, f32[5120,128]{1,0:T(8,128)S(1)}, u32[]{:S(2)}) %copy-start) | copy-done | bytes 2621464
  99.6 0.9 copy-done.3
  100.5 1.2 broadcast_in_dim.22
  101.7 4.5 %all-to-all-start.4 = ((f32[4,16,9,4,128]{4,3,2,1,0:T(4,128)}), f32[4,16,9,4,128]{4,3,2,1,0:T(4,128)}, u32[]{:S(2)}, u32[]{:S(2)}) async-start(f32[4,16,9,4,128]{4,3,2,1,0:T(4,128)} %broadcast_in_dim.22), calls=%async_computation.4 | async-start | bytes 2359296 | tf_op jit(solution)/shard_map/all_to_all | solution.py:333
  106.1 0.9 add_returned.1
  107.6 1.4 copy-done.2
  109.0 9.9 %stack_operators.1.ops_hbm = bf16[48,256,128]{2,1,0:T(8,128)(2,1)S(1)} custom-call(f32[35,35,256]{2,1,0:T(8,128)S(1)} %copy-done.2), custom_call_target="tpu_custom_call" | custom-call | flops 1000000000 | bytes 4000000 | tf_op jit(solution)/shard_map/stack_operators/pallas_call | solution.py:325
  118.9 3.5 %all-to-all-done.4 = f32[4,16,9,4,128]{4,3,2,1,0:T(4,128)} async-done(((f32[4,16,9,4,128]{4,3,2,1,0:T(4,128)}), f32[4,16,9,4,128]{4,3,2,1,0:T(4,128)}, u32[]{:S(2)}, u32[]{:S(2)}) %all-to-all-start.4) | async-done | bytes 1179680 | tf_op jit(solution)/shard_map/all_to_all | solution.py:333
  122.5 1.7 %copy-done.1 = f32[5120,128]{1,0:T(8,128)S(1)} copy-done((f32[5120,128]{1,0:T(8,128)S(1)}, f32[5120,128]{1,0:T(8,128)}, u32[]{:S(2)}) %copy-start.1) | copy-done | bytes 2621464
  124.2 1.1 copy-done.4
  125.3 11.0 %translate.1 = f32[35,64]{1,0:T(8,128)} custom-call(s32[2048]{0:T(1024)S(1)} %bitcast.17, s32[2048]{0:T(1024)S(1)} %bitcast.16, s32[128]{0:T(128)S(1)} %slice_bitcast_fusion.tile, f32[2304,128]{1,0:T(8,128)} %bitcast.11.column, bf16[48,256,128]{2,1,0:T(8,128)(2,1)S(1)} %stack_operators.1.ops_hbm, f32[5120,128]{1,0:T(8,128)S(1)} %copy-done.1, ...), custom_call_target="tpu_custom_call" | custom-call | flops 1000000000 | bytes 8000000 | tf_op jit(solution)/shard_map/translate/pallas_call | solution.py:400
  (26 shorter events, 3.0 us)
Async XLA Ops:
  0.6 70.8 %copy-start.8 = (s32[64]{0:T(128)S(1)}, s32[64]{0:T(128)}, u32[]{:S(2)}) copy-start(s32[64]{0:T(128)} %counts.5) | copy-start | bytes 772
  0.6 70.8 %copy-start.6 = (f32[64,4,128]{2,1,0:T(4,128)S(1)}, f32[64,4,128]{2,1,0:T(4,128)}, u32[]{:S(2)}) copy-start(f32[64,4,128]{2,1,0:T(4,128)} %leaves.3) | copy-start | bytes 393220
  0.7 70.8 %copy-start.10 = (s32[1,2,128]{2,1,0:T(2,128)S(1)}, s32[1,2,128]{2,1,0:T(2,128)}, u32[]{:S(2)}) copy-start(s32[1,2,128]{2,1,0:T(2,128)} %param.10) | copy-start | bytes 3076
  2.2 51.4 %all-to-all-start.2 = ((f32[8,9,2,128]{3,2,1,0:T(2,128)}), f32[8,9,2,128]{3,2,1,0:T(2,128)S(1)}, u32[]{:S(2)}, u32[]{:S(2)}) async-start(f32[8,9,2,128]{3,2,1,0:T(2,128)} %broadcast_in_dim.9), calls=%async_computation.2 | async-start | bytes 147456 | tf_op jit(solution)/shard_map/all_to_all | solution.py:333
  31.8 0.9 copy-start.5
  32.7 0.7 copy-start.7
  53.6 13.6 %all-to-all-start = ((f32[8,8,4,128]{3,2,1,0:T(4,128)}), f32[8,8,4,128]{3,2,1,0:T(4,128)S(1)}, u32[]{:S(2)}, u32[]{:S(2)}) async-start(f32[8,8,4,128]{3,2,1,0:T(4,128)} %bitcast.1), calls=%async_computation | async-start | bytes 262144 | tf_op jit(solution)/shard_map/all_to_all | solution.py:415
  68.0 20.8 %all-to-all-start.3 = ((f32[4,4,9,4,128]{4,3,2,1,0:T(4,128)}), f32[4,4,9,4,128]{4,3,2,1,0:T(4,128)S(1)}, u32[]{:S(2)}, u32[]{:S(2)}) async-start(f32[4,4,9,4,128]{4,3,2,1,0:T(4,128)} %broadcast_in_dim.10), calls=%async_computation.3 | async-start | bytes 589824 | tf_op jit(solution)/shard_map/all_to_all | solution.py:333
  71.5 21.5 %copy-start.9 = (s32[1,3,2048]{2,0,1:T(1,128)S(1)}, s32[1,3,2048]{2,0,1:T(1,128)}, u32[]{:S(2)}) copy-start(s32[1,3,2048]{2,0,1:T(1,128)} %param.12) | copy-start | bytes 73732
  88.8 11.7 %all-to-all-start.1 = ((f32[8,8,4,128]{3,2,1,0:T(4,128)}), f32[8,8,4,128]{3,2,1,0:T(4,128)S(1)}, u32[]{:S(2)}, u32[]{:S(2)}) async-start(f32[8,8,4,128]{3,2,1,0:T(4,128)} %bitcast.3), calls=%async_computation.1 | async-start | bytes 262144 | tf_op jit(solution)/shard_map/all_to_all | solution.py:417
  98.1 1.5 %copy-start = (f32[5120,128]{1,0:T(8,128)}, f32[5120,128]{1,0:T(8,128)S(1)}, u32[]{:S(2)}) copy-start(f32[5120,128]{1,0:T(8,128)S(1)} %get-tuple-element.28.slots_hbm) | copy-start | bytes 7864324
  99.6 0.9 copy-start.3
  101.7 20.8 %all-to-all-start.4 = ((f32[4,16,9,4,128]{4,3,2,1,0:T(4,128)}), f32[4,16,9,4,128]{4,3,2,1,0:T(4,128)}, u32[]{:S(2)}, u32[]{:S(2)}) async-start(f32[4,16,9,4,128]{4,3,2,1,0:T(4,128)} %broadcast_in_dim.22), calls=%async_computation.4 | async-start | bytes 2359296 | tf_op jit(solution)/shard_map/all_to_all | solution.py:333
  107.6 1.4 copy-start.2
  122.5 1.7 %copy-start.1 = (f32[5120,128]{1,0:T(8,128)S(1)}, f32[5120,128]{1,0:T(8,128)}, u32[]{:S(2)}) copy-start(f32[5120,128]{1,0:T(8,128)} %copy-done) | copy-start | bytes 7864324
  124.2 1.1 copy-start.4

commit v2 on v1

--- a/solution.py
+++ b/solution.py
@@ -14,9 +14,9 @@
 TILE = 64
 NTILE = 80
 ROWS = NTILE * TILE
-CHUNK = 8
-BATCH = 8
-MOVES = 32
+CHUNK = 16
+BATCH = 16
+MOVES = 64
 NFAR = 2048
 LEAF = 64
 PAIRS = 128
@@ -27,7 +27,7 @@
 ANY = pl.BlockSpec(memory_space=pl.ANY)
 
 
-def params(mb=32):
+def params(mb=16):
     return pltpu.CompilerParams(vmem_limit_bytes=mb * 2**20)
 
 
@@ -114,13 +114,13 @@
 
     gap = jnp.zeros((32, 128), BF16)
 
-    def forces_of(q, l, n):
-        near = jnp.concatenate([a_dist[l], a_dist[n]], axis=1)
-        dist = jnp.dot(b_dist[q], near, preferred_element_type=F32)
+    def weights(dist):
         r = lax.rsqrt(dist)
         w = r * r * r
         high = w.astype(BF16)
-        low = (w - high.astype(F32)).astype(BF16)
+        return high, (w - high.astype(F32)).astype(BF16)
+
+    def sums(q, l, n, high, low):
         sb = b_sums[q]
         sa = jnp.concatenate(
             [jnp.concatenate([a_sums[l], gap], axis=1), jnp.concatenate([gap, a_sums[n]], axis=1)], axis=0
@@ -128,6 +128,9 @@
         fb = lax.dot_general(sa, high, back, preferred_element_type=F32)
         fb = fb + lax.dot_general(sa, low, back, preferred_element_type=F32)
         fa = jnp.dot(sb, high, preferred_element_type=F32) + jnp.dot(sb, low, preferred_element_type=F32)
+        return fa, fb
+
+    def forces_of(q, l, n, fa, fb):
         bl, bn = gather_sum(fb[0:32]), gather_sum(fb[32:64])
         fl, fn = gather_sum(fa[:, 0:128]), gather_sum(fa[:, 128:256])
         back_force = bl - (b_pos[q] - a_cen[l]) * bl[3:4] + bn - (b_pos[q] - a_cen[n]) * bn[3:4]
@@ -136,9 +139,15 @@
 
     def step(c, _):
         slots = [c * BATCH + j for j in range(BATCH)]
-        leaves_of = [(named[2 * q], named[2 * q + 1]) for q in slots]
-        results = [forces_of(q, l, n) for q, (l, n) in zip(slots, leaves_of)]
-        for q, (l, n), (fb, fl, fn) in zip(slots, leaves_of, results):
+        named_by = [(q, named[2 * q], named[2 * q + 1]) for q in slots]
+        dists = [
+            jnp.dot(b_dist[q], jnp.concatenate([a_dist[l], a_dist[n]], axis=1), preferred_element_type=F32)
+            for q, l, n in named_by
+        ]
+        parts = [weights(d) for d in dists]
+        totals = [sums(*who, *part) for who, part in zip(named_by, parts)]
+        results = [forces_of(*who, *total) for who, total in zip(named_by, totals)]
+        for (q, l, n), (fb, fl, fn) in zip(named_by, results):
             slot[q] = fb
             own[l] += fl
             own[n] += fn
@@ -204,7 +213,7 @@
         rows_out[b * 128 : (b + 1) * 128, :] = jnp.concatenate([hot, where], axis=0).T
 
 
-def spread_kernel(dst, entries, select, slots, hot):
+def spread_kernel(dst, entries, sorted_out, hot):
     hot[...] = jnp.zeros_like(hot)
 
     def step(c, _):
@@ -219,8 +228,9 @@
     def turn(b, _):
         at = pl.multiple_of(b * 128, 128)
         part = hot[pl.ds(at, 128), :]
-        slots[pl.ds(at, 128), :] = jnp.where(lanes((128, 128)) < 64, pltpu.roll(part, 64, 1), part)
-        select[:, pl.ds(at, 128)] = part.T[0:64].astype(BF16)
+        spread = jnp.where(lanes((128, 128)) < 64, pltpu.roll(part, 64, 1), part)
+        sorted_out[pl.ds(at, 128), :] = spread.astype(BF16)
+        sorted_out[pl.ds(pl.multiple_of(ROWS + b * 64, 64), 64), :] = part.T[0:64].astype(BF16)
         return 0
 
     lax.fori_loop(0, ROWS // 128, turn, 0, unroll=4)
@@ -238,7 +248,7 @@
         turned = []
         for k in range(first, first + 5):
             parts = []
-            for p in split_rows(ops[:, k, :]):
+            for p in split_rows(ops[k]):
                 parts += [p, pad]
             flat = jnp.concatenate(parts + [tail], axis=0).astype(BF16)
             turned.append(lax.dot_general(same, flat, (((1,), (1,)), ((), ())), preferred_element_type=F32))
@@ -255,12 +265,10 @@
     lax.fori_loop(0, NGROUP // 4, narrow, 0)
 
 
-def far_kernel(row, dst, tile, column, ops_hbm, slots_hbm, select_hbm, out,
-               ops, slots, select, table, picked, sems):
+def far_kernel(row, dst, tile, column, ops_hbm, places_hbm, out, ops, places, table, picked, sems):
     copies = [
         pltpu.make_async_copy(ops_hbm, ops, sems.at[0]),
-        pltpu.make_async_copy(slots_hbm, slots, sems.at[1]),
-        pltpu.make_async_copy(select_hbm, select, sems.at[2]),
+        pltpu.make_async_copy(places_hbm, places, sems.at[1]),
     ]
     for c in copies:
         c.start()
@@ -299,18 +307,22 @@
 
     def translate(c, total):
         at = pl.multiple_of(c * (CHUNK * TILE), CHUNK * TILE)
-        out_rows = []
+        lefts = []
         for j in range(CHUNK):
             here = pl.ds(pl.multiple_of(at + j * TILE, TILE), TILE)
             x = picked[here, :]
-            s = slots[here, :]
+            s = places[here, :].astype(F32)
             xl = split(jnp.where(s == left, x, 0.0))
             xr = split(jnp.where(s == right, x, 0.0))
-            lhs = jnp.concatenate([jnp.concatenate([a, b], axis=1) for a, b in zip(xl, xr)], axis=0)
-            y = jnp.dot(lhs, ops[tile[c * CHUNK + j]], preferred_element_type=F32)
-            out_rows.append(y[0:TILE] + y[TILE : 2 * TILE] + y[2 * TILE :])
-        moved = split(jnp.concatenate(out_rows, axis=0))
-        chosen = select[:, pl.ds(at, CHUNK * TILE)]
+            lefts.append(jnp.concatenate([jnp.concatenate([a, b], axis=1) for a, b in zip(xl, xr)], axis=0))
+        ys = [
+            jnp.dot(lhs, ops[tile[c * CHUNK + j]], preferred_element_type=F32) for j, lhs in enumerate(lefts)
+        ]
+        moved = split(jnp.concatenate([y[0:TILE] + y[TILE : 2 * TILE] + y[2 * TILE :] for y in ys], axis=0))
+        blocks = CHUNK * TILE // 128
+        chosen = jnp.concatenate(
+            [places[pl.ds(pl.multiple_of(ROWS + (c * blocks + b) * 64, 64), 64), :] for b in range(blocks)], axis=1
+        )
         for part in moved:
             total = total + jnp.dot(chosen, part, preferred_element_type=F32)
         return total
@@ -326,7 +338,7 @@
         stack_kernel, out_shape=jax.ShapeDtypeStruct((NGROUP, 256, 128), BF16),
         in_specs=[VMEM], out_specs=VMEM, scratch_shapes=[pltpu.VMEM((NGROUP, 264, 128), F32)],
         compiler_params=params(), cost_estimate=cost(10**9, 4 * 10**6), name="stack_operators",
-    )(trans_ops)
+    )(jnp.transpose(trans_ops, (1, 0, 2)))
 
 
 def spread_out(block, axes, n):
@@ -336,7 +348,7 @@
 def first_stage(multipoles):
     block = jnp.pad(multipoles, ((0, 1), (0, 0))).reshape(9, 2, 128)
     block = spread_out(block, "u", 8)
-    return block.reshape(4, 2, 36, 64).transpose(0, 2, 1, 3).reshape(4, 9, 4, 128)
+    return block.reshape(4, 2, 36, 64).transpose(0, 2, 1, 3).reshape(144, 128)
 
 
 def cost(flops, size):
@@ -386,44 +398,45 @@
         cost_estimate=cost(10**8, 10**5), name="class_order",
     )(far.reshape(3, 16, 128))
     dst = dst.reshape(NFAR)
-    select, slots = pl.pallas_call(
+    places = pl.pallas_call(
         spread_kernel,
-        out_shape=[jax.ShapeDtypeStruct((64, ROWS), BF16), jax.ShapeDtypeStruct((ROWS, 128), F32)],
-        in_specs=[SMEM, VMEM], out_specs=[VMEM] * 2,
+        out_shape=jax.ShapeDtypeStruct((ROWS + ROWS // 2, 128), BF16),
+        in_specs=[SMEM, VMEM], out_specs=VMEM,
         scratch_shapes=[pltpu.VMEM((ROWS, 128), F32)], compiler_params=params(),
         cost_estimate=cost(10**9, 4 * 10**6), name="sorted_targets",
     )(dst, entries)
-    return dst, row.reshape(NFAR), tile[0], select, slots
-
-
-def far_last(dst, row, tile, select, slots, ops, column):
+    return dst, row.reshape(NFAR), tile[0], places
+
+
+def far_last(dst, row, tile, places, ops, column):
     return pl.pallas_call(
         far_kernel, out_shape=jax.ShapeDtypeStruct((NCOEF, 64), F32),
-        in_specs=[SMEM, SMEM, SMEM, VMEM, ANY, ANY, ANY], out_specs=VMEM,
+        in_specs=[SMEM, SMEM, SMEM, VMEM, ANY, ANY], out_specs=VMEM,
         scratch_shapes=[
-            pltpu.VMEM((NGROUP, 256, 128), BF16), pltpu.VMEM((ROWS, 128), F32), pltpu.VMEM((64, ROWS), BF16),
+            pltpu.VMEM((NGROUP, 256, 128), BF16), pltpu.VMEM((ROWS + ROWS // 2, 128), BF16),
             pltpu.VMEM((TABLE, 128), F32), pltpu.VMEM((ROWS, 128), F32),
-            pltpu.SemaphoreType.DMA((3,)),
+            pltpu.SemaphoreType.DMA((2,)),
         ],
-        compiler_params=params(40), cost_estimate=cost(10**9, 8 * 10**6), name="translate",
-    )(row, dst, tile, column, ops, slots, select)
+        compiler_params=params(20), cost_estimate=cost(10**9, 8 * 10**6), name="translate",
+    )(row, dst, tile, column, ops, places)
 
 
 def shards(leaves, counts, send_list, pair_list, multipoles, far_list, trans_ops):
     send = send_list.reshape(64)
+    block = first_stage(multipoles)
+    block, far_list = lax.optimization_barrier((block, far_list))
     outgoing = near_first(leaves, counts, send).reshape(8, 8, 4, 128)
     received = lax.all_to_all(outgoing, "grp", 0, 0, tiled=True).reshape(64, 4, 128)
+    dst, row, tile, places = far_order(far_list[0])
     own, slot = near_pairs(leaves, counts, pair_list.reshape(2 * PAIRS), received)
+    block = spread_out(block, "v", 4).reshape(576, 128)
+    block, slot, trans_ops = lax.optimization_barrier((block, slot, trans_ops))
     back = lax.all_to_all(slot.reshape(8, 8, 4, 128), "grp", 0, 0, tiled=True).reshape(64, 4, 128)
+    ops = stacked_ops(trans_ops)
+    block, back, ops = lax.optimization_barrier((block, back, ops))
+    block = spread_out(block, "x", 4)
     forces = near_last(counts, send, own, back)
-    block = first_stage(multipoles)
-    block, far_list = lax.optimization_barrier((block, far_list))
-    block = spread_out(block, "v", 4).reshape(16, 9, 4, 128)
-    dst, row, tile, select, slots = far_order(far_list[0])
-    block, trans_ops, slots, select = lax.optimization_barrier((block, trans_ops, slots, select))
-    block = spread_out(block, "x", 4)
-    ops = stacked_ops(trans_ops)
-    local = far_last(dst, row, tile, select, slots, ops, block.reshape(64 * 36, 128))
+    local = far_last(dst, row, tile, places, ops, block.reshape(64 * 36, 128))
     return forces, local
 
 

time: 137 us -> 126 us (0.920); the launches traced: 136 us -> 124 us
  Pallas kernels: 45.6 us -> 29.6 us
  waiting for transfers between devices: 27.3 us -> 32.5 us
  local copies, waits for them, and re-layouts: 13.3 us -> 10.9 us
    pallas_call x1, Pallas kernels: 17.3 us -> 8.59 us  [near_pairs(): pl.pallas_call(pair_kernel, out_shape=[jax.ShapeDtypeStruct((LEAF, 4, 128...]
    pallas_call x1, Pallas kernels: 9.92 us -> 4.31 us  [stacked_ops(): pl.pallas_call(stack_kernel, out_shape=jax.ShapeDtypeStruct((NGROUP, 256,...]
    all_to_all x3, waiting for transfers between devices: 22.4 us -> 27.1 us  [spread_out(): lax.all_to_all(jnp.broadcast_to(block[None], (n,) + block.shape), axes, 0...]
    unnamed x23 -> x21, local copies, waits for them, and re-layouts: 8.78 us -> 5.07 us
  transfers between devices with their start and end apart: 5 -> 5, of which waited for: 3 -> 4; matrix products, arithmetic and copies ran while one was open for 1% -> 2% of each run, Pallas kernels for 25% -> 16%
where the time goes in v2:
time: 126 us; the launch traced here: 124 us
  starting transfers between devices  50.3 us (40%)
  waiting for transfers between devices  32.5 us (26%)
  Pallas kernels  29.6 us (23%)
  local copies, waits for them, and re-layouts  10.9 us (9%)
    all_to_all x3, starting transfers between devices, spread_out(): lax.all_to_all(jnp.broadcast_to(block[None], (n,) + block.shape), axes, 0...  36.7 us
    all_to_all x3, waiting for transfers between devices, spread_out(): lax.all_to_all(jnp.broadcast_to(block[None], (n,) + block.shape), axes, 0...  27.1 us
    pallas_call x1, Pallas kernels, far_last(): pl.pallas_call(far_kernel, out_shape=jax.ShapeDtypeStruct((NCOEF, 64), F3...  9.91 us
    pallas_call x1, Pallas kernels, near_pairs(): pl.pallas_call(pair_kernel, out_shape=[jax.ShapeDtypeStruct((LEAF, 4, 128...  8.59 us
    all_to_all x1, starting transfers between devices, shards(): lax.all_to_all(outgoing, 'grp', 0, 0, tiled=True).reshape(64, 4, 128)  8.36 us
    all_to_all x1, starting transfers between devices, shards(): lax.all_to_all(slot.reshape(8, 8, 4, 128), 'grp', 0, 0, tiled=True)  5.17 us
    unnamed x21, local copies, waits for them, and re-layouts  5.07 us
    all_to_all x1, waiting for transfers between devices, shards(): lax.all_to_all(outgoing, 'grp', 0, 0, tiled=True).reshape(64, 4, 128)  4.91 us
  transfers between devices with their start and end apart: 5, of which 4 were waited for; matrix products, arithmetic and copies ran while one was open for 2% of the time, Pallas kernels for 16%

profile of v2, /device:TPU:1, one launch (start us, length us, event | category | flops | bytes accessed | tf_op | source)
XLA Modules:
  0.0 124.1 jit_solution(3250399616051577375)
XLA Ops:
  0.7 0.8 pad.4
  1.5 0.7 broadcast_in_dim.9
  2.2 28.9 %all-to-all-start.1 = ((f32[8,9,2,128]{3,2,1,0:T(2,128)}), f32[8,9,2,128]{3,2,1,0:T(2,128)S(1)}, u32[]{:S(2)}, u32[]{:S(2)}) async-start(f32[8,9,2,128]{3,2,1,0:T(2,128)} %broadcast_in_dim.9), calls=%async_computation.1 | async-start | bytes 147456 | tf_op jit(solution)/shard_map/all_to_all | solution.py:345
  31.1 0.8 reshape.43.send
  31.8 0.9 copy-done.2
  32.7 0.7 copy-done.4
  33.4 1.3 %pack_blocks.1 = f32[64,4,128]{2,1,0:T(4,128)} custom-call(f32[64,4,128]{2,1,0:T(4,128)S(1)} %copy-done.2, s32[64]{0:T(128)S(1)} %copy-done.4, s32[64]{0:T(128)S(1)} %reshape.43.send), custom_call_target="tpu_custom_call" | custom-call | flops 1000000 | bytes 1000000 | tf_op jit(solution)/shard_map/pack_blocks/pallas_call | solution.py:359
  34.7 18.9 %all-to-all-done.1 = f32[8,9,2,128]{3,2,1,0:T(2,128)S(1)} async-done(((f32[8,9,2,128]{3,2,1,0:T(2,128)}), f32[8,9,2,128]{3,2,1,0:T(2,128)S(1)}, u32[]{:S(2)}, u32[]{:S(2)}) %all-to-all-start.1) | async-done | bytes 73760 | tf_op jit(solution)/shard_map/all_to_all | solution.py:345
  53.6 8.4 %all-to-all-start = ((f32[8,8,4,128]{3,2,1,0:T(4,128)}), f32[8,8,4,128]{3,2,1,0:T(4,128)S(1)}, u32[]{:S(2)}, u32[]{:S(2)}) async-start(f32[8,8,4,128]{3,2,1,0:T(4,128)} %bitcast.1), calls=%async_computation | async-start | bytes 262144 | tf_op jit(solution)/shard_map/all_to_all | solution.py:429
  62.3 4.9 %all-to-all-done = f32[8,8,4,128]{3,2,1,0:T(4,128)S(1)} async-done(((f32[8,8,4,128]{3,2,1,0:T(4,128)}), f32[8,8,4,128]{3,2,1,0:T(4,128)S(1)}, u32[]{:S(2)}, u32[]{:S(2)}) %all-to-all-start) | async-done | bytes 131104 | tf_op jit(solution)/shard_map/all_to_all | solution.py:429
  67.2 0.7 broadcast_in_dim.10
  68.0 3.5 %all-to-all-start.2 = ((f32[4,144,128]{2,1,0:T(8,128)}), f32[4,144,128]{2,1,0:T(8,128)S(1)}, u32[]{:S(2)}, u32[]{:S(2)}) async-start(f32[4,144,128]{2,1,0:T(8,128)} %broadcast_in_dim.10), calls=%async_computation.2 | async-start | bytes 589824 | tf_op jit(solution)/shard_map/all_to_all | solution.py:345
  71.5 8.6 %pair_forces.1 = (f32[64,4,128]{2,1,0:T(4,128)S(1)}, f32[64,4,128]{2,1,0:T(4,128)}) custom-call(s32[256]{0:T(256)S(1)} %bitcast.23, s32[64]{0:T(128)S(1)} %copy-done.5, f32[64,4,128]{2,1,0:T(4,128)S(1)} %copy-done.3, f32[64,4,128]{2,1,0:T(4,128)S(1)} %bitcast.18), custom_call_target="tpu_custom_call" | custom-call | flops 1000000000 | bytes 4000000 | tf_op jit(solution)/shard_map/pair_forces/pallas_call | solution.py:367
  80.1 5.2 %all-to-all-start.3 = ((f32[8,8,4,128]{3,2,1,0:T(4,128)}), f32[8,8,4,128]{3,2,1,0:T(4,128)S(1)}, u32[]{:S(2)}, u32[]{:S(2)}) async-start(f32[8,8,4,128]{3,2,1,0:T(4,128)} %bitcast.5), calls=%async_computation.3 | async-start | bytes 262144 | tf_op jit(solution)/shard_map/all_to_all | solution.py:434
  85.7 4.3 %stack_operators.1.ops_hbm = bf16[48,256,128]{2,1,0:T(8,128)(2,1)S(1)} custom-call(f32[35,35,256]{2,1,0:T(8,128)S(1)} %bitcast.16), custom_call_target="tpu_custom_call" | custom-call | flops 1000000000 | bytes 4000000 | tf_op jit(solution)/shard_map/stack_operators/pallas_call | solution.py:337
  90.5 2.0 %broadcast_in_dim.22 = f32[4,576,128]{2,1,0:T(8,128)} broadcast(f32[576,128]{1,0:T(8,128)} %bitcast.24), dimensions={1,2} | broadcast | bytes 1474560 | tf_op jit(solution)/shard_map/broadcast_in_dim | solution.py:345
  92.6 4.4 %all-to-all-start.4 = ((f32[4,576,128]{2,1,0:T(8,128)}), f32[4,576,128]{2,1,0:T(8,128)}, u32[]{:S(2)}, u32[]{:S(2)}) async-start(f32[4,576,128]{2,1,0:T(8,128)} %broadcast_in_dim.22), calls=%async_computation.4 | async-start | bytes 2359296 | tf_op jit(solution)/shard_map/all_to_all | solution.py:345
  97.5 4.1 %sorted_targets.1.places_hbm = bf16[7680,128]{1,0:T(8,128)(2,1)S(1)} custom-call(s32[2048]{0:T(1024)S(1)} %bitcast.19, f32[2048,128]{1,0:T(8,128)S(1)} %get-tuple-element.29.entries), custom_call_target="tpu_custom_call" | custom-call | flops 1000000000 | bytes 4000000 | tf_op jit(solution)/shard_map/sorted_targets/pallas_call | solution.py:401
  101.7 1.3 %copy-done = bf16[7680,128]{1,0:T(8,128)(2,1)} copy-done((bf16[7680,128]{1,0:T(8,128)(2,1)}, bf16[7680,128]{1,0:T(8,128)(2,1)S(1)}, u32[]{:S(2)}) %copy-start) | copy-done | bytes 1966104
  102.9 0.9 add_returned.1
  103.8 0.6 copy.15
  104.5 8.2 %all-to-all-done.4 = f32[4,576,128]{2,1,0:T(8,128)} async-done(((f32[4,576,128]{2,1,0:T(8,128)}), f32[4,576,128]{2,1,0:T(8,128)}, u32[]{:S(2)}, u32[]{:S(2)}) %all-to-all-start.4) | async-done | bytes 1179680 | tf_op jit(solution)/shard_map/all_to_all | solution.py:345
  112.7 1.5 %copy-done.1 = bf16[7680,128]{1,0:T(8,128)(2,1)S(1)} copy-done((bf16[7680,128]{1,0:T(8,128)(2,1)S(1)}, bf16[7680,128]{1,0:T(8,128)(2,1)}, u32[]{:S(2)}) %copy-start.1) | copy-done | bytes 1966104
  114.2 9.9 %translate.1 = f32[35,64]{1,0:T(8,128)} custom-call(s32[2048]{0:T(1024)S(1)} %bitcast.21, s32[2048]{0:T(1024)S(1)} %bitcast.20, s32[128]{0:T(128)S(1)} %slice_bitcast_fusion.tile, f32[2304,128]{1,0:T(8,128)} %bitcast.12.column, bf16[48,256,128]{2,1,0:T(8,128)(2,1)S(1)} %stack_operators.1.ops_hbm, bf16[7680,128]{1,0:T(8,128)(2,1)S(1)} %copy-done.1), custom_call_target="tpu_custom_call" | custom-call | flops 1000000000 | bytes 8000000 | tf_op jit(solution)/shard_map/translate/pallas_call | solution.py:412
  (25 shorter events, 2.0 us)
Async XLA Ops:
  0.6 70.8 %copy-start.5 = (s32[64]{0:T(128)S(1)}, s32[64]{0:T(128)}, u32[]{:S(2)}) copy-start(s32[64]{0:T(128)} %counts.5) | copy-start | bytes 772
  0.6 70.8 %copy-start.3 = (f32[64,4,128]{2,1,0:T(4,128)S(1)}, f32[64,4,128]{2,1,0:T(4,128)}, u32[]{:S(2)}) copy-start(f32[64,4,128]{2,1,0:T(4,128)} %leaves.3) | copy-start | bytes 393220
  0.7 70.8 %copy-start.7 = (s32[1,2,128]{2,1,0:T(2,128)S(1)}, s32[1,2,128]{2,1,0:T(2,128)}, u32[]{:S(2)}) copy-start(s32[1,2,128]{2,1,0:T(2,128)} %param.10) | copy-start | bytes 3076
  2.2 51.4 %all-to-all-start.1 = ((f32[8,9,2,128]{3,2,1,0:T(2,128)}), f32[8,9,2,128]{3,2,1,0:T(2,128)S(1)}, u32[]{:S(2)}, u32[]{:S(2)}) async-start(f32[8,9,2,128]{3,2,1,0:T(2,128)} %broadcast_in_dim.9), calls=%async_computation.1 | async-start | bytes 147456 | tf_op jit(solution)/shard_map/all_to_all | solution.py:345
  31.8 0.9 copy-start.2
  32.7 0.7 copy-start.4
  53.6 13.6 %all-to-all-start = ((f32[8,8,4,128]{3,2,1,0:T(4,128)}), f32[8,8,4,128]{3,2,1,0:T(4,128)S(1)}, u32[]{:S(2)}, u32[]{:S(2)}) async-start(f32[8,8,4,128]{3,2,1,0:T(4,128)} %bitcast.1), calls=%async_computation | async-start | bytes 262144 | tf_op jit(solution)/shard_map/all_to_all | solution.py:429
  68.0 12.1 %all-to-all-start.2 = ((f32[4,144,128]{2,1,0:T(8,128)}), f32[4,144,128]{2,1,0:T(8,128)S(1)}, u32[]{:S(2)}, u32[]{:S(2)}) async-start(f32[4,144,128]{2,1,0:T(8,128)} %broadcast_in_dim.10), calls=%async_computation.2 | async-start | bytes 589824 | tf_op jit(solution)/shard_map/all_to_all | solution.py:345
  71.4 13.8 %copy-start.8 = (f32[35,35,256]{2,1,0:T(8,128)S(1)}, f32[35,35,256]{2,1,0:T(8,128)}, u32[]{:S(2)}) copy-start(f32[35,35,256]{2,1,0:T(8,128)} %param.13) | copy-start | bytes 3763204
  80.1 5.6 %copy-start.9 = (f32[4,144,128]{2,1,0:T(8,128)}, f32[4,144,128]{2,1,0:T(8,128)S(1)}, u32[]{:S(2)}) copy-start(f32[4,144,128]{2,1,0:T(8,128)S(1)} %all-to-all-done.2) | copy-start | bytes 884740
  80.1 10.5 %all-to-all-start.3 = ((f32[8,8,4,128]{3,2,1,0:T(4,128)}), f32[8,8,4,128]{3,2,1,0:T(4,128)S(1)}, u32[]{:S(2)}, u32[]{:S(2)}) async-start(f32[8,8,4,128]{3,2,1,0:T(4,128)} %bitcast.5), calls=%async_computation.3 | async-start | bytes 262144 | tf_op jit(solution)/shard_map/all_to_all | solution.py:434
  92.6 4.4 %copy-start.6 = (s32[1,3,2048]{2,0,1:T(1,128)S(1)}, s32[1,3,2048]{2,0,1:T(1,128)}, u32[]{:S(2)}) copy-start(s32[1,3,2048]{2,0,1:T(1,128)} %param.12) | copy-start | bytes 73732
  92.6 20.1 %all-to-all-start.4 = ((f32[4,576,128]{2,1,0:T(8,128)}), f32[4,576,128]{2,1,0:T(8,128)}, u32[]{:S(2)}, u32[]{:S(2)}) async-start(f32[4,576,128]{2,1,0:T(8,128)} %broadcast_in_dim.22), calls=%async_computation.4 | async-start | bytes 2359296 | tf_op jit(solution)/shard_map/all_to_all | solution.py:345
  101.7 1.3 %copy-start = (bf16[7680,128]{1,0:T(8,128)(2,1)}, bf16[7680,128]{1,0:T(8,128)(2,1)S(1)}, u32[]{:S(2)}) copy-start(bf16[7680,128]{1,0:T(8,128)(2,1)S(1)} %sorted_targets.1.places_hbm) | copy-start | bytes 5898244
  112.7 1.5 %copy-start.1 = (bf16[7680,128]{1,0:T(8,128)(2,1)S(1)}, bf16[7680,128]{1,0:T(8,128)(2,1)}, u32[]{:S(2)}) copy-start(bf16[7680,128]{1,0:T(8,128)(2,1)} %copy-done) | copy-start | bytes 5898244

commit v3 on v2

--- a/solution.py
+++ b/solution.py
@@ -24,7 +24,6 @@
 
 VMEM = pl.BlockSpec(memory_space=pltpu.VMEM)
 SMEM = pl.BlockSpec(memory_space=pltpu.SMEM)
-ANY = pl.BlockSpec(memory_space=pl.ANY)
 
 
 def params(mb=16):
@@ -156,7 +155,7 @@
     lax.fori_loop(0, LEAF // BATCH, step, 0)
 
 
-def finish_kernel(counts, send, own, back, out, total):
+def finish_kernel(counts, send, own, back, ready, out, total):
     total[...] = own[...]
 
     def add(k, _):
@@ -213,8 +212,9 @@
         rows_out[b * 128 : (b + 1) * 128, :] = jnp.concatenate([hot, where], axis=0).T
 
 
-def spread_kernel(dst, entries, sorted_out, hot):
+def spread_kernel(dst, entries, sorted_out, ready, hot):
     hot[...] = jnp.zeros_like(hot)
+    ready[...] = jnp.zeros_like(ready)
 
     def step(c, _):
         some = [c * MOVES + j for j in range(MOVES)]
@@ -265,14 +265,7 @@
     lax.fori_loop(0, NGROUP // 4, narrow, 0)
 
 
-def far_kernel(row, dst, tile, column, ops_hbm, places_hbm, out, ops, places, table, picked, sems):
-    copies = [
-        pltpu.make_async_copy(ops_hbm, ops, sems.at[0]),
-        pltpu.make_async_copy(places_hbm, places, sems.at[1]),
-    ]
-    for c in copies:
-        c.start()
-
+def far_kernel(row, dst, tile, column, ops, places, out, table, picked):
     pad = jnp.zeros((4, 128), F32)
     tail = jnp.zeros((8, 128), F32)
 
@@ -297,8 +290,6 @@
         return 0
 
     lax.fori_loop(0, NFAR // MOVES, pick, 0)
-    for c in copies:
-        c.wait()
 
     lane = lanes((TILE, 128))
     place = (lane >= STRIDE).astype(F32) + (lane >= 2 * STRIDE).astype(F32) + 1.0
@@ -380,13 +371,13 @@
     )(pairs, counts, leaves, received)
 
 
-def near_last(counts, send, own, back):
+def near_last(counts, send, own, back, ready):
     return pl.pallas_call(
         finish_kernel, out_shape=jax.ShapeDtypeStruct((LEAF, 3, 128), F32),
-        in_specs=[SMEM, SMEM, VMEM, VMEM], out_specs=VMEM,
+        in_specs=[SMEM, SMEM, VMEM, VMEM, VMEM], out_specs=VMEM,
         scratch_shapes=[pltpu.VMEM((LEAF, 4, 128), F32)], compiler_params=params(),
         cost_estimate=cost(10**6, 10**6), name="add_returned",
-    )(counts, send, own, back)
+    )(counts, send, own, back, ready)
 
 
 def far_order(far):
@@ -398,25 +389,21 @@
         cost_estimate=cost(10**8, 10**5), name="class_order",
     )(far.reshape(3, 16, 128))
     dst = dst.reshape(NFAR)
-    places = pl.pallas_call(
+    places, ready = pl.pallas_call(
         spread_kernel,
-        out_shape=jax.ShapeDtypeStruct((ROWS + ROWS // 2, 128), BF16),
-        in_specs=[SMEM, VMEM], out_specs=VMEM,
+        out_shape=[jax.ShapeDtypeStruct((ROWS + ROWS // 2, 128), BF16), jax.ShapeDtypeStruct((8, 128), F32)],
+        in_specs=[SMEM, VMEM], out_specs=[VMEM] * 2,
         scratch_shapes=[pltpu.VMEM((ROWS, 128), F32)], compiler_params=params(),
         cost_estimate=cost(10**9, 4 * 10**6), name="sorted_targets",
     )(dst, entries)
-    return dst, row.reshape(NFAR), tile[0], places
+    return dst, row.reshape(NFAR), tile[0], places, ready
 
 
 def far_last(dst, row, tile, places, ops, column):
     return pl.pallas_call(
         far_kernel, out_shape=jax.ShapeDtypeStruct((NCOEF, 64), F32),
-        in_specs=[SMEM, SMEM, SMEM, VMEM, ANY, ANY], out_specs=VMEM,
-        scratch_shapes=[
-            pltpu.VMEM((NGROUP, 256, 128), BF16), pltpu.VMEM((ROWS + ROWS // 2, 128), BF16),
-            pltpu.VMEM((TABLE, 128), F32), pltpu.VMEM((ROWS, 128), F32),
-            pltpu.SemaphoreType.DMA((2,)),
-        ],
+        in_specs=[SMEM, SMEM, SMEM, VMEM, VMEM, VMEM], out_specs=VMEM,
+        scratch_shapes=[pltpu.VMEM((TABLE, 128), F32), pltpu.VMEM((ROWS, 128), F32)],
         compiler_params=params(20), cost_estimate=cost(10**9, 8 * 10**6), name="translate",
     )(row, dst, tile, column, ops, places)
 
@@ -424,19 +411,20 @@
 def shards(leaves, counts, send_list, pair_list, multipoles, far_list, trans_ops):
     send = send_list.reshape(64)
     block = first_stage(multipoles)
-    block, far_list = lax.optimization_barrier((block, far_list))
+    block, far_list, trans_ops = lax.optimization_barrier((block, far_list, trans_ops))
     outgoing = near_first(leaves, counts, send).reshape(8, 8, 4, 128)
     received = lax.all_to_all(outgoing, "grp", 0, 0, tiled=True).reshape(64, 4, 128)
-    dst, row, tile, places = far_order(far_list[0])
+    ops = stacked_ops(trans_ops)
+    block, received, ops = lax.optimization_barrier((block, received, ops))
     own, slot = near_pairs(leaves, counts, pair_list.reshape(2 * PAIRS), received)
     block = spread_out(block, "v", 4).reshape(576, 128)
-    block, slot, trans_ops = lax.optimization_barrier((block, slot, trans_ops))
+    block, far_list, own, slot = lax.optimization_barrier((block, far_list, own, slot))
+    dst, row, tile, places, ready = far_order(far_list[0])
+    block = spread_out(block, "x", 4)
+    block, slot, ready = lax.optimization_barrier((block, slot, ready))
     back = lax.all_to_all(slot.reshape(8, 8, 4, 128), "grp", 0, 0, tiled=True).reshape(64, 4, 128)
-    ops = stacked_ops(trans_ops)
-    block, back, ops = lax.optimization_barrier((block, back, ops))
-    block = spread_out(block, "x", 4)
-    forces = near_last(counts, send, own, back)
     local = far_last(dst, row, tile, places, ops, block.reshape(64 * 36, 128))
+    forces = near_last(counts, send, own, back, ready)
     return forces, local
 
 

time: 126 us -> 124 us (0.984)
  waiting for transfers between devices: 32.5 us -> 29.8 us
  local copies, waits for them, and re-layouts: 10.9 us -> 12.2 us
    all_to_all x1, waiting for transfers between devices: 4.91 us -> 0.01 us  [shards(): lax.all_to_all(outgoing, 'grp', 0, 0, tiled=True).reshape(64, 4, 128)]
    all_to_all x3, waiting for transfers between devices: 27.1 us -> 29.8 us  [spread_out(): lax.all_to_all(jnp.broadcast_to(block[None], (n,) + block.shape), axes, 0...]
    optimization_barrier x1, local copies, waits for them, and re-layouts: 0.42 us -> 1.78 us  [shards(): lax.optimization_barrier((block, far_list, trans_ops))]
    unnamed x21 -> x17, local copies, waits for them, and re-layouts: 5.07 us -> 5.06 us
  transfers between devices with their start and end apart: 5 -> 5, of which waited for: 4 -> 3; matrix products, arithmetic and copies ran while one was open for 2% -> 2% of each run, Pallas kernels for 16% -> 23%
where the time goes in v3:
time: 124 us; the launch traced here: 123 us
  starting transfers between devices  50.8 us (41%)
  waiting for transfers between devices  29.8 us (24%)
  Pallas kernels  29.2 us (24%)
  local copies, waits for them, and re-layouts  12.2 us (10%)
    all_to_all x3, starting transfers between devices, spread_out(): lax.all_to_all(jnp.broadcast_to(block[None], (n,) + block.shape), axes, 0...  37.4 us
    all_to_all x3, waiting for transfers between devices, spread_out(): lax.all_to_all(jnp.broadcast_to(block[None], (n,) + block.shape), axes, 0...  29.8 us
    pallas_call x1, Pallas kernels, far_last(): pl.pallas_call(far_kernel, out_shape=jax.ShapeDtypeStruct((NCOEF, 64), F3...  9.48 us
    pallas_call x1, Pallas kernels, near_pairs(): pl.pallas_call(pair_kernel, out_shape=[jax.ShapeDtypeStruct((LEAF, 4, 128...  8.6 us
    all_to_all x1, starting transfers between devices, shards(): lax.all_to_all(outgoing, 'grp', 0, 0, tiled=True).reshape(64, 4, 128)  8.36 us
    unnamed x17, local copies, waits for them, and re-layouts  5.06 us
    all_to_all x1, starting transfers between devices, shards(): lax.all_to_all(slot.reshape(8, 8, 4, 128), 'grp', 0, 0, tiled=True)  5.03 us
    pallas_call x1, Pallas kernels, stacked_ops(): pl.pallas_call(stack_kernel, out_shape=jax.ShapeDtypeStruct((NGROUP, 256,...  4.31 us
  transfers between devices with their start and end apart: 5, of which 3 were waited for; matrix products, arithmetic and copies ran while one was open for 2% of the time, Pallas kernels for 23%

profile of v3, /device:TPU:1, one launch (start us, length us, event | category | flops | bytes accessed | tf_op | source)
XLA Modules:
  0.0 122.8 jit_solution(15743647298235026839)
XLA Ops:
  0.6 0.7 pad.4
  1.4 0.7 broadcast_in_dim.9
  2.1 28.9 %all-to-all-start = ((f32[8,9,2,128]{3,2,1,0:T(2,128)}), f32[8,9,2,128]{3,2,1,0:T(2,128)S(1)}, u32[]{:S(2)}, u32[]{:S(2)}) async-start(f32[8,9,2,128]{3,2,1,0:T(2,128)} %broadcast_in_dim.9), calls=%async_computation | async-start | bytes 147456 | tf_op jit(solution)/shard_map/all_to_all | solution.py:336
  31.0 0.8 reshape.43.send
  31.8 0.9 copy-done.2
  32.7 0.7 copy-done.4
  33.3 1.3 %pack_blocks.1 = f32[64,4,128]{2,1,0:T(4,128)} custom-call(f32[64,4,128]{2,1,0:T(4,128)S(1)} %copy-done.2, s32[64]{0:T(128)S(1)} %copy-done.4, s32[64]{0:T(128)S(1)} %reshape.43.send), custom_call_target="tpu_custom_call" | custom-call | flops 1000000 | bytes 1000000 | tf_op jit(solution)/shard_map/pack_blocks/pallas_call | solution.py:350
  34.7 18.9 %all-to-all-done = f32[8,9,2,128]{3,2,1,0:T(2,128)S(1)} async-done(((f32[8,9,2,128]{3,2,1,0:T(2,128)}), f32[8,9,2,128]{3,2,1,0:T(2,128)S(1)}, u32[]{:S(2)}, u32[]{:S(2)}) %all-to-all-start) | async-done | bytes 73760 | tf_op jit(solution)/shard_map/all_to_all | solution.py:336
  53.5 8.4 %all-to-all-start.1 = ((f32[8,8,4,128]{3,2,1,0:T(4,128)}), f32[8,8,4,128]{3,2,1,0:T(4,128)S(1)}, u32[]{:S(2)}, u32[]{:S(2)}) async-start(f32[8,8,4,128]{3,2,1,0:T(4,128)} %bitcast.1), calls=%async_computation.1 | async-start | bytes 262144 | tf_op jit(solution)/shard_map/all_to_all | solution.py:416
  62.2 1.8 %copy.17 = f32[35,35,256]{2,0,1:T(8,128)S(1)} copy(f32[35,35,256]{2,1,0:T(8,128)} %param.13) | data formatting | bytes 2508800 | tf_op jit(solution)/shard_map/optimization_barrier | solution.py:414
  64.1 4.3 %stack_operators.1.ops = bf16[48,256,128]{2,1,0:T(8,128)(2,1)S(1)} custom-call(f32[35,35,256]{2,1,0:T(8,128)S(1)} %bitcast.16), custom_call_target="tpu_custom_call" | custom-call | flops 1000000000 | bytes 4000000 | tf_op jit(solution)/shard_map/stack_operators/pallas_call | solution.py:328
  68.4 0.7 broadcast_in_dim.10
  69.1 4.1 %all-to-all-start.2 = ((f32[4,144,128]{2,1,0:T(8,128)}), f32[4,144,128]{2,1,0:T(8,128)}, u32[]{:S(2)}, u32[]{:S(2)}) async-start(f32[4,144,128]{2,1,0:T(8,128)} %broadcast_in_dim.10), calls=%async_computation.2 | async-start | bytes 589824 | tf_op jit(solution)/shard_map/all_to_all | solution.py:336
  73.3 8.6 %pair_forces.1 = (f32[64,4,128]{2,1,0:T(4,128)S(1)}, f32[64,4,128]{2,1,0:T(4,128)}) custom-call(s32[256]{0:T(256)S(1)} %bitcast.23, s32[64]{0:T(128)S(1)} %copy-done.5, f32[64,4,128]{2,1,0:T(4,128)S(1)} %copy-done.3, f32[64,4,128]{2,1,0:T(4,128)S(1)} %bitcast.18), custom_call_target="tpu_custom_call" | custom-call | flops 1000000000 | bytes 4000000 | tf_op jit(solution)/shard_map/pair_forces/pallas_call | solution.py:358
  81.9 1.2 all-to-all-done.2
  83.0 2.1 %broadcast_in_dim.22 = f32[4,576,128]{2,1,0:T(8,128)} broadcast(f32[576,128]{1,0:T(8,128)} %bitcast.4), dimensions={1,2} | broadcast | bytes 1474560 | tf_op jit(solution)/shard_map/broadcast_in_dim | solution.py:336
  85.1 4.4 %all-to-all-start.3 = ((f32[4,576,128]{2,1,0:T(8,128)}), f32[4,576,128]{2,1,0:T(8,128)}, u32[]{:S(2)}, u32[]{:S(2)}) async-start(f32[4,576,128]{2,1,0:T(8,128)} %broadcast_in_dim.22), calls=%async_computation.3 | async-start | bytes 2359296 | tf_op jit(solution)/shard_map/all_to_all | solution.py:336
  90.0 4.1 %sorted_targets.1 = (bf16[7680,128]{1,0:T(8,128)(2,1)S(1)}, f32[8,128]{1,0:T(8,128)S(1)}) custom-call(s32[2048]{0:T(1024)S(1)} %bitcast.19, f32[2048,128]{1,0:T(8,128)S(1)} %get-tuple-element.35.entries), custom_call_target="tpu_custom_call" | custom-call | flops 1000000000 | bytes 4000000 | tf_op jit(solution)/shard_map/sorted_targets/pallas_call | solution.py:392
  94.2 1.3 %copy-done = bf16[7680,128]{1,0:T(8,128)(2,1)} copy-done((bf16[7680,128]{1,0:T(8,128)(2,1)}, bf16[7680,128]{1,0:T(8,128)(2,1)S(1)}, u32[]{:S(2)}) %copy-start) | copy-done | bytes 1966104
  95.5 9.8 %all-to-all-done.3 = f32[4,576,128]{2,1,0:T(8,128)} async-done(((f32[4,576,128]{2,1,0:T(8,128)}), f32[4,576,128]{2,1,0:T(8,128)}, u32[]{:S(2)}, u32[]{:S(2)}) %all-to-all-start.3) | async-done | bytes 1179680 | tf_op jit(solution)/shard_map/all_to_all | solution.py:336
  105.3 5.0 %all-to-all-start.4 = ((f32[8,8,4,128]{3,2,1,0:T(4,128)}), f32[8,8,4,128]{3,2,1,0:T(4,128)S(1)}, u32[]{:S(2)}, u32[]{:S(2)}) async-start(f32[8,8,4,128]{3,2,1,0:T(4,128)} %bitcast.8), calls=%async_computation.4 | async-start | bytes 262144 | tf_op jit(solution)/shard_map/all_to_all | solution.py:425
  110.3 1.5 %copy-done.1 = bf16[7680,128]{1,0:T(8,128)(2,1)S(1)} copy-done((bf16[7680,128]{1,0:T(8,128)(2,1)S(1)}, bf16[7680,128]{1,0:T(8,128)(2,1)}, u32[]{:S(2)}) %copy-start.1) | copy-done | bytes 1966104
  111.8 9.5 %translate.1 = f32[35,64]{1,0:T(8,128)} custom-call(s32[2048]{0:T(1024)S(1)} %bitcast.21, s32[2048]{0:T(1024)S(1)} %bitcast.20, s32[128]{0:T(128)S(1)} %slice_bitcast_fusion.tile, f32[2304,128]{1,0:T(8,128)} %bitcast.12.column, bf16[48,256,128]{2,1,0:T(8,128)(2,1)S(1)} %stack_operators.1.ops, bf16[7680,128]{1,0:T(8,128)(2,1)S(1)} %copy-done.1), custom_call_target="tpu_custom_call" | custom-call | flops 1000000000 | bytes 8000000 | tf_op jit(solution)/shard_map/translate/pallas_call | solution.py:403
  121.3 0.9 add_returned.1
  (21 shorter events, 1.6 us)
Async XLA Ops:
  2.1 51.4 %all-to-all-start = ((f32[8,9,2,128]{3,2,1,0:T(2,128)}), f32[8,9,2,128]{3,2,1,0:T(2,128)S(1)}, u32[]{:S(2)}, u32[]{:S(2)}) async-start(f32[8,9,2,128]{3,2,1,0:T(2,128)} %broadcast_in_dim.9), calls=%async_computation | async-start | bytes 147456 | tf_op jit(solution)/shard_map/all_to_all | solution.py:336
  31.8 0.9 copy-start.2
  32.7 0.7 copy-start.4
  53.5 14.9 %all-to-all-start.1 = ((f32[8,8,4,128]{3,2,1,0:T(4,128)}), f32[8,8,4,128]{3,2,1,0:T(4,128)S(1)}, u32[]{:S(2)}, u32[]{:S(2)}) async-start(f32[8,8,4,128]{3,2,1,0:T(4,128)} %bitcast.1), calls=%async_computation.1 | async-start | bytes 262144 | tf_op jit(solution)/shard_map/all_to_all | solution.py:416
  64.0 9.2 %copy-start.3 = (f32[64,4,128]{2,1,0:T(4,128)S(1)}, f32[64,4,128]{2,1,0:T(4,128)}, u32[]{:S(2)}) copy-start(f32[64,4,128]{2,1,0:T(4,128)} %leaves.3) | copy-start | bytes 393220
  64.0 9.2 %copy-start.5 = (s32[64]{0:T(128)S(1)}, s32[64]{0:T(128)}, u32[]{:S(2)}) copy-start(s32[64]{0:T(128)} %counts.5) | copy-start | bytes 772
  64.1 9.2 %copy-start.7 = (s32[1,2,128]{2,1,0:T(2,128)S(1)}, s32[1,2,128]{2,1,0:T(2,128)}, u32[]{:S(2)}) copy-start(s32[1,2,128]{2,1,0:T(2,128)} %param.10) | copy-start | bytes 3076
  69.1 13.9 %all-to-all-start.2 = ((f32[4,144,128]{2,1,0:T(8,128)}), f32[4,144,128]{2,1,0:T(8,128)}, u32[]{:S(2)}, u32[]{:S(2)}) async-start(f32[4,144,128]{2,1,0:T(8,128)} %broadcast_in_dim.10), calls=%async_computation.2 | async-start | bytes 589824 | tf_op jit(solution)/shard_map/all_to_all | solution.py:336
  85.1 4.4 %copy-start.6 = (s32[1,3,2048]{2,0,1:T(1,128)S(1)}, s32[1,3,2048]{2,0,1:T(1,128)}, u32[]{:S(2)}) copy-start(s32[1,3,2048]{2,0,1:T(1,128)} %param.12) | copy-start | bytes 73732
  85.1 20.2 %all-to-all-start.3 = ((f32[4,576,128]{2,1,0:T(8,128)}), f32[4,576,128]{2,1,0:T(8,128)}, u32[]{:S(2)}, u32[]{:S(2)}) async-start(f32[4,576,128]{2,1,0:T(8,128)} %broadcast_in_dim.22), calls=%async_computation.3 | async-start | bytes 2359296 | tf_op jit(solution)/shard_map/all_to_all | solution.py:336
  94.2 1.3 %copy-start = (bf16[7680,128]{1,0:T(8,128)(2,1)}, bf16[7680,128]{1,0:T(8,128)(2,1)S(1)}, u32[]{:S(2)}) copy-start(bf16[7680,128]{1,0:T(8,128)(2,1)S(1)} %get-tuple-element.43.places) | copy-start | bytes 5898244
  105.3 16.1 %all-to-all-start.4 = ((f32[8,8,4,128]{3,2,1,0:T(4,128)}), f32[8,8,4,128]{3,2,1,0:T(4,128)S(1)}, u32[]{:S(2)}, u32[]{:S(2)}) async-start(f32[8,8,4,128]{3,2,1,0:T(4,128)} %bitcast.8), calls=%async_computation.4 | async-start | bytes 262144 | tf_op jit(solution)/shard_map/all_to_all | solution.py:425
  110.3 1.5 %copy-start.1 = (bf16[7680,128]{1,0:T(8,128)(2,1)S(1)}, bf16[7680,128]{1,0:T(8,128)(2,1)}, u32[]{:S(2)}) copy-start(bf16[7680,128]{1,0:T(8,128)(2,1)} %copy-done) | copy-start | bytes 5898244

commit v4 on v3

--- a/solution.py
+++ b/solution.py
@@ -155,7 +155,7 @@
     lax.fori_loop(0, LEAF // BATCH, step, 0)
 
 
-def finish_kernel(counts, send, own, back, ready, out, total):
+def finish_kernel(counts, send, own, back, out, total):
     total[...] = own[...]
 
     def add(k, _):
@@ -236,7 +236,7 @@
     lax.fori_loop(0, ROWS // 128, turn, 0, unroll=4)
 
 
-def stack_kernel(ops, out, stacked):
+def stack_kernel(ops, ready, out, stacked):
     stacked[:, 104:256, :] = jnp.zeros((NGROUP, 152, 128), F32)
     pad = jnp.zeros((STRIDE - NCOEF, 256), F32)
     tail = jnp.zeros((128 - 3 * STRIDE, 256), F32)
@@ -324,12 +324,12 @@
     out[...] = flat[0:NCOEF] + flat[STRIDE : STRIDE + NCOEF] + flat[2 * STRIDE : 2 * STRIDE + NCOEF]
 
 
-def stacked_ops(trans_ops):
+def stacked_ops(trans_ops, ready):
     return pl.pallas_call(
         stack_kernel, out_shape=jax.ShapeDtypeStruct((NGROUP, 256, 128), BF16),
-        in_specs=[VMEM], out_specs=VMEM, scratch_shapes=[pltpu.VMEM((NGROUP, 264, 128), F32)],
+        in_specs=[VMEM] * 2, out_specs=VMEM, scratch_shapes=[pltpu.VMEM((NGROUP, 264, 128), F32)],
         compiler_params=params(), cost_estimate=cost(10**9, 4 * 10**6), name="stack_operators",
-    )(jnp.transpose(trans_ops, (1, 0, 2)))
+    )(jnp.transpose(trans_ops, (1, 0, 2)), ready)
 
 
 def spread_out(block, axes, n):
@@ -371,13 +371,13 @@
     )(pairs, counts, leaves, received)
 
 
-def near_last(counts, send, own, back, ready):
+def near_last(counts, send, own, back):
     return pl.pallas_call(
         finish_kernel, out_shape=jax.ShapeDtypeStruct((LEAF, 3, 128), F32),
-        in_specs=[SMEM, SMEM, VMEM, VMEM, VMEM], out_specs=VMEM,
+        in_specs=[SMEM, SMEM, VMEM, VMEM], out_specs=VMEM,
         scratch_shapes=[pltpu.VMEM((LEAF, 4, 128), F32)], compiler_params=params(),
         cost_estimate=cost(10**6, 10**6), name="add_returned",
-    )(counts, send, own, back, ready)
+    )(counts, send, own, back)
 
 
 def far_order(far):
@@ -411,20 +411,21 @@
 def shards(leaves, counts, send_list, pair_list, multipoles, far_list, trans_ops):
     send = send_list.reshape(64)
     block = first_stage(multipoles)
-    block, far_list, trans_ops = lax.optimization_barrier((block, far_list, trans_ops))
     outgoing = near_first(leaves, counts, send).reshape(8, 8, 4, 128)
+    block, outgoing = lax.optimization_barrier((block, outgoing))
     received = lax.all_to_all(outgoing, "grp", 0, 0, tiled=True).reshape(64, 4, 128)
-    ops = stacked_ops(trans_ops)
-    block, received, ops = lax.optimization_barrier((block, received, ops))
+    block, received = lax.optimization_barrier((block, received))
     own, slot = near_pairs(leaves, counts, pair_list.reshape(2 * PAIRS), received)
     block = spread_out(block, "v", 4).reshape(576, 128)
-    block, far_list, own, slot = lax.optimization_barrier((block, far_list, own, slot))
+    block, far_list, trans_ops, own, slot = lax.optimization_barrier((block, far_list, trans_ops, own, slot))
     dst, row, tile, places, ready = far_order(far_list[0])
+    trans_ops, ready = lax.optimization_barrier((trans_ops, ready))
+    ops = stacked_ops(trans_ops, ready)
     block = spread_out(block, "x", 4)
-    block, slot, ready = lax.optimization_barrier((block, slot, ready))
+    block, slot, ops = lax.optimization_barrier((block, slot, ops))
     back = lax.all_to_all(slot.reshape(8, 8, 4, 128), "grp", 0, 0, tiled=True).reshape(64, 4, 128)
     local = far_last(dst, row, tile, places, ops, block.reshape(64 * 36, 128))
-    forces = near_last(counts, send, own, back, ready)
+    forces = near_last(counts, send, own, back)
     return forces, local
 
 

time: 124 us -> 120 us (0.968)
  blocking collectives: 0 us -> 13.4 us
  starting transfers between devices: 50.8 us -> 42.9 us
  waiting for transfers between devices: 29.8 us -> 23.4 us
  local copies, waits for them, and re-layouts: 12.2 us -> 9.96 us
    all_to_all x0 -> x1, blocking collectives: none -> 13.4 us  [shards(): lax.all_to_all(outgoing, 'grp', 0, 0, tiled=True).reshape(64, 4, 128)]
    all_to_all x1 -> x0, starting transfers between devices: 8.36 us -> none  [shards(): lax.all_to_all(outgoing, 'grp', 0, 0, tiled=True).reshape(64, 4, 128)]
    all_to_all x3, waiting for transfers between devices: 29.8 us -> 23.4 us  [spread_out(): lax.all_to_all(jnp.broadcast_to(block[None], (n,) + block.shape), axes, 0...]
    optimization_barrier x1, local copies, waits for them, and re-layouts: 1.78 us -> 0.42 us  [shards(): trans_ops, ready = lax.optimization_barrier((trans_ops, ready))]
    unnamed x17 -> x19, local copies, waits for them, and re-layouts: 5.06 us -> 5.06 us
  transfers between devices with their start and end apart: 5 -> 4, of which waited for: 3 -> 2; matrix products, arithmetic and copies ran while one was open for 2% -> 1% of each run, Pallas kernels for 23% -> 23%
where the time goes in v4:
time: 120 us; the launch traced here: 119 us
  starting transfers between devices  42.9 us (36%)
  Pallas kernels  28.6 us (24%)
  waiting for transfers between devices  23.4 us (20%)
  blocking collectives  13.4 us (11%)
  local copies, waits for them, and re-layouts  9.96 us (8%)
    all_to_all x3, starting transfers between devices, spread_out(): lax.all_to_all(jnp.broadcast_to(block[None], (n,) + block.shape), axes, 0...  36.7 us
    all_to_all x3, waiting for transfers between devices, spread_out(): lax.all_to_all(jnp.broadcast_to(block[None], (n,) + block.shape), axes, 0...  23.4 us
    all_to_all x1, blocking collectives, shards(): lax.all_to_all(outgoing, 'grp', 0, 0, tiled=True).reshape(64, 4, 128)  13.4 us
    pallas_call x1, Pallas kernels, far_last(): pl.pallas_call(far_kernel, out_shape=jax.ShapeDtypeStruct((NCOEF, 64), F3...  9.45 us
    pallas_call x1, Pallas kernels, near_pairs(): pl.pallas_call(pair_kernel, out_shape=[jax.ShapeDtypeStruct((LEAF, 4, 128...  8.62 us
    all_to_all x1, starting transfers between devices, shards(): lax.all_to_all(slot.reshape(8, 8, 4, 128), 'grp', 0, 0, tiled=True)  6.15 us
    unnamed x19, local copies, waits for them, and re-layouts  5.06 us
    pallas_call x1, Pallas kernels, stacked_ops(): pl.pallas_call(stack_kernel, out_shape=jax.ShapeDtypeStruct((NGROUP, 256,...  4.31 us
  transfers between devices with their start and end apart: 4, of which 2 were waited for; matrix products, arithmetic and copies ran while one was open for 1% of the time, Pallas kernels for 23%

profile of v4, /device:TPU:1, one launch (start us, length us, event | category | flops | bytes accessed | tf_op | source)
XLA Modules:
  0.0 119.0 jit_solution(17741684709974767539)
XLA Ops:
  0.7 0.8 pad.4
  1.5 0.7 broadcast_in_dim.9
  2.2 28.9 %all-to-all-start = ((f32[8,9,2,128]{3,2,1,0:T(2,128)}), f32[8,9,2,128]{3,2,1,0:T(2,128)S(1)}, u32[]{:S(2)}, u32[]{:S(2)}) async-start(f32[8,9,2,128]{3,2,1,0:T(2,128)} %broadcast_in_dim.9), calls=%async_computation | async-start | bytes 147456 | tf_op jit(solution)/shard_map/all_to_all | solution.py:336
  31.1 0.8 reshape.43.send
  31.9 0.9 copy-done.2
  32.8 0.7 copy-done.4
  33.4 0.7 pack_blocks.1
  34.1 19.5 %all-to-all-done = f32[8,9,2,128]{3,2,1,0:T(2,128)S(1)} async-done(((f32[8,9,2,128]{3,2,1,0:T(2,128)}), f32[8,9,2,128]{3,2,1,0:T(2,128)S(1)}, u32[]{:S(2)}, u32[]{:S(2)}) %all-to-all-start) | async-done | bytes 73760 | tf_op jit(solution)/shard_map/all_to_all | solution.py:336
  54.0 13.4 %all_to_all.25 = f32[8,8,4,128]{3,2,1,0:T(4,128)S(1)} all-to-all(f32[8,8,4,128]{3,2,1,0:T(4,128)S(1)} %bitcast.18), channel_id=1, replica_groups=mesh['u'=8,'v'=4,'x'=4,'grp'=8] {'grp'}, dimensions={0} | all-to-all | bytes 262144 | tf_op jit(solution)/shard_map/all_to_all | solution.py:416
  67.4 0.7 broadcast_in_dim.10
  68.1 3.5 %all-to-all-start.2 = ((f32[4,144,128]{2,1,0:T(8,128)}), f32[4,144,128]{2,1,0:T(8,128)S(1)}, u32[]{:S(2)}, u32[]{:S(2)}) async-start(f32[4,144,128]{2,1,0:T(8,128)} %broadcast_in_dim.10), calls=%async_computation.2 | async-start | bytes 589824 | tf_op jit(solution)/shard_map/all_to_all | solution.py:336
  71.6 8.6 %pair_forces.1 = (f32[64,4,128]{2,1,0:T(4,128)S(1)}, f32[64,4,128]{2,1,0:T(4,128)}) custom-call(s32[256]{0:T(256)S(1)} %bitcast.24, s32[64]{0:T(128)S(1)} %copy-done.5, f32[64,4,128]{2,1,0:T(4,128)S(1)} %copy-done.3, f32[64,4,128]{2,1,0:T(4,128)S(1)} %bitcast.19), custom_call_target="tpu_custom_call" | custom-call | flops 1000000000 | bytes 4000000 | tf_op jit(solution)/shard_map/pair_forces/pallas_call | solution.py:358
  80.2 1.1 broadcast_in_dim.22
  81.3 4.4 %all-to-all-start.3 = ((f32[4,576,128]{2,1,0:T(8,128)}), f32[4,576,128]{2,1,0:T(8,128)}, u32[]{:S(2)}, u32[]{:S(2)}) async-start(f32[4,576,128]{2,1,0:T(8,128)} %broadcast_in_dim.22), calls=%async_computation.3 | async-start | bytes 2359296 | tf_op jit(solution)/shard_map/all_to_all | solution.py:336
  85.7 0.5 class_order.1
  86.3 4.1 %sorted_targets.1 = (bf16[7680,128]{1,0:T(8,128)(2,1)S(1)}, f32[8,128]{1,0:T(8,128)S(1)}) custom-call(s32[2048]{0:T(1024)S(1)} %bitcast.20, f32[2048,128]{1,0:T(8,128)S(1)} %get-tuple-element.36.entries), custom_call_target="tpu_custom_call" | custom-call | flops 1000000000 | bytes 4000000 | tf_op jit(solution)/shard_map/sorted_targets/pallas_call | solution.py:392
  90.4 1.3 %copy-done = bf16[7680,128]{1,0:T(8,128)(2,1)} copy-done((bf16[7680,128]{1,0:T(8,128)(2,1)}, bf16[7680,128]{1,0:T(8,128)(2,1)S(1)}, u32[]{:S(2)}) %copy-start) | copy-done | bytes 1966104
  92.1 4.3 %stack_operators.1.ops = bf16[48,256,128]{2,1,0:T(8,128)(2,1)S(1)} custom-call(f32[35,35,256]{2,1,0:T(8,128)S(1)} %bitcast.16, f32[8,128]{1,0:T(8,128)S(1)} %get-tuple-element.39.ready), custom_call_target="tpu_custom_call" | custom-call | flops 1000000000 | bytes 4000000 | tf_op jit(solution)/shard_map/stack_operators/pallas_call | solution.py:328
  96.5 3.9 %all-to-all-done.3 = f32[4,576,128]{2,1,0:T(8,128)} async-done(((f32[4,576,128]{2,1,0:T(8,128)}), f32[4,576,128]{2,1,0:T(8,128)}, u32[]{:S(2)}, u32[]{:S(2)}) %all-to-all-start.3) | async-done | bytes 1179680 | tf_op jit(solution)/shard_map/all_to_all | solution.py:336
  100.4 6.2 %all-to-all-start.4 = ((f32[8,8,4,128]{3,2,1,0:T(4,128)}), f32[8,8,4,128]{3,2,1,0:T(4,128)S(1)}, u32[]{:S(2)}, u32[]{:S(2)}) async-start(f32[8,8,4,128]{3,2,1,0:T(4,128)} %bitcast.8), calls=%async_computation.4 | async-start | bytes 262144 | tf_op jit(solution)/shard_map/all_to_all | solution.py:426
  106.5 1.5 %copy-done.1 = bf16[7680,128]{1,0:T(8,128)(2,1)S(1)} copy-done((bf16[7680,128]{1,0:T(8,128)(2,1)S(1)}, bf16[7680,128]{1,0:T(8,128)(2,1)}, u32[]{:S(2)}) %copy-start.1) | copy-done | bytes 1966104
  108.1 9.5 %translate.1 = f32[35,64]{1,0:T(8,128)} custom-call(s32[2048]{0:T(1024)S(1)} %bitcast.22, s32[2048]{0:T(1024)S(1)} %bitcast.21, s32[128]{0:T(128)S(1)} %slice_bitcast_fusion.tile, f32[2304,128]{1,0:T(8,128)} %bitcast.12.column, bf16[48,256,128]{2,1,0:T(8,128)(2,1)S(1)} %stack_operators.1.ops, bf16[7680,128]{1,0:T(8,128)(2,1)S(1)} %copy-done.1), custom_call_target="tpu_custom_call" | custom-call | flops 1000000000 | bytes 8000000 | tf_op jit(solution)/shard_map/translate/pallas_call | solution.py:403
  117.5 0.9 add_returned.1
  118.4 0.6 copy.15
  (22 shorter events, 0.9 us)
Async XLA Ops:
  0.6 71.0 %copy-start.3 = (f32[64,4,128]{2,1,0:T(4,128)S(1)}, f32[64,4,128]{2,1,0:T(4,128)}, u32[]{:S(2)}) copy-start(f32[64,4,128]{2,1,0:T(4,128)} %leaves.3) | copy-start | bytes 393220
  0.6 71.0 %copy-start.5 = (s32[64]{0:T(128)S(1)}, s32[64]{0:T(128)}, u32[]{:S(2)}) copy-start(s32[64]{0:T(128)} %counts.5) | copy-start | bytes 772
  0.7 71.0 %copy-start.7 = (s32[1,2,128]{2,1,0:T(2,128)S(1)}, s32[1,2,128]{2,1,0:T(2,128)}, u32[]{:S(2)}) copy-start(s32[1,2,128]{2,1,0:T(2,128)} %param.10) | copy-start | bytes 3076
  2.2 51.4 %all-to-all-start = ((f32[8,9,2,128]{3,2,1,0:T(2,128)}), f32[8,9,2,128]{3,2,1,0:T(2,128)S(1)}, u32[]{:S(2)}, u32[]{:S(2)}) async-start(f32[8,9,2,128]{3,2,1,0:T(2,128)} %broadcast_in_dim.9), calls=%async_computation | async-start | bytes 147456 | tf_op jit(solution)/shard_map/all_to_all | solution.py:336
  31.8 0.9 copy-start.2
  32.8 0.7 copy-start.4
  68.1 12.1 %all-to-all-start.2 = ((f32[4,144,128]{2,1,0:T(8,128)}), f32[4,144,128]{2,1,0:T(8,128)S(1)}, u32[]{:S(2)}, u32[]{:S(2)}) async-start(f32[4,144,128]{2,1,0:T(8,128)} %broadcast_in_dim.10), calls=%async_computation.2 | async-start | bytes 589824 | tf_op jit(solution)/shard_map/all_to_all | solution.py:336
  81.3 4.4 %copy-start.6 = (s32[1,3,2048]{2,0,1:T(1,128)S(1)}, s32[1,3,2048]{2,0,1:T(1,128)}, u32[]{:S(2)}) copy-start(s32[1,3,2048]{2,0,1:T(1,128)} %param.12) | copy-start | bytes 73732
  81.3 19.0 %all-to-all-start.3 = ((f32[4,576,128]{2,1,0:T(8,128)}), f32[4,576,128]{2,1,0:T(8,128)}, u32[]{:S(2)}, u32[]{:S(2)}) async-start(f32[4,576,128]{2,1,0:T(8,128)} %broadcast_in_dim.22), calls=%async_computation.3 | async-start | bytes 2359296 | tf_op jit(solution)/shard_map/all_to_all | solution.py:336
  86.3 5.4 %copy-start.8 = (f32[35,35,256]{2,1,0:T(8,128)S(1)}, f32[35,35,256]{2,1,0:T(8,128)}, u32[]{:S(2)}) copy-start(f32[35,35,256]{2,1,0:T(8,128)} %param.13) | copy-start | bytes 3763204
  90.4 1.3 %copy-start = (bf16[7680,128]{1,0:T(8,128)(2,1)}, bf16[7680,128]{1,0:T(8,128)(2,1)S(1)}, u32[]{:S(2)}) copy-start(bf16[7680,128]{1,0:T(8,128)(2,1)S(1)} %get-tuple-element.45.places) | copy-start | bytes 5898244
  100.4 17.2 %all-to-all-start.4 = ((f32[8,8,4,128]{3,2,1,0:T(4,128)}), f32[8,8,4,128]{3,2,1,0:T(4,128)S(1)}, u32[]{:S(2)}, u32[]{:S(2)}) async-start(f32[8,8,4,128]{3,2,1,0:T(4,128)} %bitcast.8), calls=%async_computation.4 | async-start | bytes 262144 | tf_op jit(solution)/shard_map/all_to_all | solution.py:426
  106.5 1.5 %copy-start.1 = (bf16[7680,128]{1,0:T(8,128)(2,1)S(1)}, bf16[7680,128]{1,0:T(8,128)(2,1)}, u32[]{:S(2)}) copy-start(bf16[7680,128]{1,0:T(8,128)(2,1)} %copy-done) | copy-start | bytes 5898244
